TPU v7x, 32 devices: a whole 2x2x4 slice. The times are simulated.
32 devices in a mesh: grp: 2 (over y), lat: 4 (over z), lon: 2 (over x), role: 2 (over core).
Axes of the slice: x: 2, y: 2, z: 4, core: 2. Of those that a mesh axis runs over, the one named last changes fastest.
Arguments:
- eastern_edge_current: float32 [8, 128, 256], P('lon', ('grp', 'lat', 'role')), parts along dimension 1, may hold values from -1.5 to 1.5
- northern_edge_current: float32 [8, 128, 256], P('lon', ('grp', 'lat', 'role')), parts along dimension 1, may hold values from -1.5 to 1.5
- thermal_anomaly: float32 [8, 128, 256], P('lon', ('grp', 'lat', 'role')), parts along dimension 1, may hold values from -6 to 6
- prior_warming: float32 [8, 128, 256], P('lon', ('grp', 'lat', 'role')), parts along dimension 1, may hold values from 0 to 0.5
- solute_fields: float32 [24, 8, 128, 256], P(None, None, ('grp', 'lat', 'role'), 'lon'), parts along dimension 2, may hold values from -6 to 6
- submerged_layer_count: int32 [128, 256], P(('grp', 'lat', 'role')), parts along dimension 0, may hold values from 0 to 8
- reaction_rates: float32 [24, 24], replicated, may hold values from -1.25 to 1.25
Outputs:
- u_out: float32 [8, 128, 256], P('lon', ('grp', 'lat', 'role')), parts along dimension 1
- v_out: float32 [8, 128, 256], P('lon', ('grp', 'lat', 'role')), parts along dimension 1
- temp_out: float32 [8, 128, 256], P('lon', ('grp', 'lat', 'role')), parts along dimension 1
- heating_out: float32 [8, 128, 256], P('lon', ('grp', 'lat', 'role')), parts along dimension 1
- tracers_out: float32 [24, 8, 128, 256], P(None, None, ('grp', 'lat', 'role'), 'lon'), parts along dimension 2
There are 2 independent parts, one for each index of `grp`. A program takes and returns all parts, laid end to end along the dimension named above; an argument that names none is the same for every part. Nothing has to cross between parts.
All inputs are finite; a program needn't handle non-finite values.
Results may differ from a plain program's by a relative error of at most 0.0001.
Values sent between devices are 32-bit elements; how exact they have to be, the bound alone decides.
A program may use at most 64 MiB of HBM per device.

v0:
```python
import jax
import jax.numpy as jnp
from jax import lax
from jax.sharding import PartitionSpec as P

DEPTH_LAYERS = 8
STEPS = 2


def padded(shard, sides, width):
    for axis, dim in sides:
        count, length = (lax.axis_size(axis), shard.shape[dim])
        up = [(i, (i + 1) % count) for i in range(count - 1)]
        down = [(j, i) for i, j in up]
        last = lax.slice_in_dim(shard, length - width, length, axis=dim)
        leading = lax.slice_in_dim(shard, 0, width, axis=dim)
        before = lax.ppermute(last, axis, up)
        after = lax.ppermute(leading, axis, down)
        shard = jnp.concatenate([before, shard, after], axis=dim)
    return shard


def passed_along(shard, axis, by):
    count = lax.axis_size(axis)
    pairs = [(i, i + by) for i in range(count) if 0 <= i + by < count]
    return lax.ppermute(shard, axis, pairs)


def flow_advance(extended, wet_ext, thermal_energy, coriolis_parameter):

    def inner(q):
        return q[..., 1:-1, 1:-1]

    def east_of(q):
        return q[..., 1:-1, 2:]

    def west_of(q):
        return q[..., 1:-1, :-2]

    def north_of(q):
        return q[..., 2:, 1:-1]

    def south_of(q):
        return q[..., :-2, 1:-1]

    def diffusion_operator(q):
        return east_of(q) + west_of(q) + north_of(q) + south_of(q) - 4.0 * inner(q)

    u_ext, v_ext, temp_ext = (extended[0], extended[1], extended[2])
    ocean_mask = inner(wet_ext)
    ocean_mask_eastward = ocean_mask * east_of(wet_ext)
    ocean_mask_poleward = ocean_mask * north_of(wet_ext)
    u_here, v_here, temp_here = (inner(u_ext), inner(v_ext), inner(temp_ext))
    updated_eastward_flow = ocean_mask_eastward * (
        u_here
        + 0.1 * diffusion_operator(u_ext)
        + 0.3 * coriolis_parameter * v_here
        - 0.2 * (east_of(temp_ext) - temp_here)
    )
    updated_poleward_flow = ocean_mask_poleward * (
        v_here
        + 0.1 * diffusion_operator(v_ext)
        - 0.3 * coriolis_parameter * u_here
        - 0.2 * (north_of(temp_ext) - temp_here)
    )
    temp_new = ocean_mask * (temp_here + 0.1 * diffusion_operator(temp_ext) + 0.5 * thermal_energy)
    return (updated_eastward_flow, updated_poleward_flow, temp_new)


def tracer_step(solute_fields, faces, ocean_mask, reaction_rates):
    count = solute_fields.shape[0]
    layered_bundle = jnp.concatenate([solute_fields, faces], axis=0)
    extended = padded(layered_bundle, ((("lat", "role"), 2), ("lon", 3)), 1)
    solute_amount = extended[:count]
    east_u = extended[count]
    north_v = extended[count + 1]
    face_u = east_u[:, 1:-1, :-1]
    flux_x = (
        jnp.maximum(face_u, 0.0) * solute_amount[:, :, 1:-1, :-1]
        + jnp.minimum(face_u, 0.0) * solute_amount[:, :, 1:-1, 1:]
    )
    face_v = north_v[:, :-1, 1:-1]
    flux_y = (
        jnp.maximum(face_v, 0.0) * solute_amount[:, :, :-1, 1:-1]
        + jnp.minimum(face_v, 0.0) * solute_amount[:, :, 1:, 1:-1]
    )
    here = solute_amount[:, :, 1:-1, 1:-1]
    advected = here - 0.5 * (
        flux_x[..., 1:] - flux_x[..., :-1] + (flux_y[..., 1:, :] - flux_y[..., :-1, :])
    )
    atten = 0.1 + 0.3 * jnp.maximum(advected[0], 0.0)
    summed = jnp.cumsum(atten, axis=0)
    depth_tau = jnp.concatenate([jnp.zeros_like(atten[:1]), summed[:-1]], axis=0)
    top = jnp.exp(-depth_tau)
    thermal_energy = 2.0 * ocean_mask * (top - jnp.exp(-(depth_tau + atten)))
    react = jnp.einsum("ab,bzyx->azyx", reaction_rates, advected, precision=lax.Precision.HIGHEST)
    return (ocean_mask * (advected + 0.5 * top * react), thermal_energy)


def shards(
    eastern_edge_current,
    northern_edge_current,
    thermal_anomaly,
    prior_warming,
    solute_fields,
    submerged_layer_count,
    reaction_rates,
):
    level_share = eastern_edge_current.shape[0]
    rows = eastern_edge_current.shape[1]
    width = solute_fields.shape[3]
    strip = lax.axis_index(("lat", "role"))
    column = lax.axis_index("lon")
    total_rows = rows * lax.axis_size(("lat", "role"))
    row_ids = (strip * rows + jnp.arange(rows, dtype=jnp.int32)).astype(jnp.float32)
    coriolis_parameter = (2.0 * (row_ids + 0.5) / total_rows - 1.0)[:, None]
    northern_row = passed_along(submerged_layer_count[:1], ("lat", "role"), -1)
    depth_ext = jnp.concatenate(
        [jnp.zeros_like(submerged_layer_count[:1]), submerged_layer_count, northern_row], axis=0
    )
    depth_pad = jnp.pad(depth_ext, ((0, 0), (1, 1)))
    tile_depth = lax.dynamic_slice_in_dim(depth_pad, column * width, width + 2, 1)
    all_levels = jnp.arange(DEPTH_LAYERS, dtype=jnp.int32)
    wet_tile_ext = (all_levels[:, None, None] < tile_depth[None, :, :]).astype(jnp.float32)
    wet_tile = wet_tile_ext[:, 1:-1, 1:-1]
    solute_amount = solute_fields
    own_levels = column * level_share + jnp.arange(level_share, dtype=jnp.int32)
    wet_strip_ext = (own_levels[:, None, None] < depth_pad[None, :, :]).astype(jnp.float32)
    eastward_current, poleward_current, seawater_warmth, thermal_energy = (
        eastern_edge_current,
        northern_edge_current,
        thermal_anomaly,
        prior_warming,
    )
    for step in range(STEPS):
        layered_bundle = jnp.stack([eastward_current, poleward_current, seawater_warmth])
        extended = padded(layered_bundle, ((("lat", "role"), 2),), 1)
        extended = jnp.pad(extended, ((0, 0), (0, 0), (0, 0), (1, 1)))
        eastward_current, poleward_current, seawater_warmth = flow_advance(
            extended, wet_strip_ext, thermal_energy, coriolis_parameter
        )
        faces = lax.all_to_all(
            jnp.stack([eastward_current, poleward_current]),
            "lon",
            split_axis=3,
            concat_axis=1,
            tiled=True,
        )
        solute_amount, heat_tile = tracer_step(solute_amount, faces, wet_tile, reaction_rates)
        thermal_energy = lax.all_to_all(heat_tile, "lon", split_axis=0, concat_axis=2, tiled=True)
    return (eastward_current, poleward_current, seawater_warmth, thermal_energy, solute_amount)


def solution(mesh):
    return jax.shard_map(
        shards,
        mesh=mesh,
        in_specs=(
            P("lon", ("grp", "lat", "role"), None),
            P("lon", ("grp", "lat", "role"), None),
            P("lon", ("grp", "lat", "role"), None),
            P("lon", ("grp", "lat", "role"), None),
            P(None, None, ("grp", "lat", "role"), "lon"),
            P(("grp", "lat", "role"), None),
            P(),
        ),
        out_specs=(
            P("lon", ("grp", "lat", "role"), None),
            P("lon", ("grp", "lat", "role"), None),
            P("lon", ("grp", "lat", "role"), None),
            P("lon", ("grp", "lat", "role"), None),
            P(None, None, ("grp", "lat", "role"), "lon"),
        ),
        check_vma=False,
    )
```

profile of v0, /device:TPU:0, one launch (start us, length us, event | category | flops | bytes accessed | tf_op | source)
XLA Modules:
  0.0 117.5 jit_solution(12957497192411766998)
XLA Ops:
  1.4 1.3 %collective-permute-start = (s32[1,256]{1,0:T(1,128)S(1)}, s32[1,256]{1,0:T(1,128)S(1)}, u32[]{:S(2)}, u32[]{:S(2)}) collective-permute-start(s32[1,256]{1,0:T(1,128)S(1)} %slice.289), channel_id=1, source_target_pairs={{1,0},{4,1},{5,4},{8,5},{9,8},{12,9},{13,12},{3,2},{6,3},{7,6},{10... | collective-permute-start | bytes 3080 | tf_op jit(solution)/shard_map/ppermute | solution.py:26
  3.5 3.0 %collective-permute-start.1 = (f32[3,4,1,256]{3,1,2,0:T(4,128)S(1)}, f32[3,4,1,256]{3,1,2,0:T(4,128)S(1)}, u32[]{:S(2)}, u32[]{:S(2)}) collective-permute-start(f32[3,4,1,256]{3,1,2,0:T(4,128)S(1)} %get-tuple-element.62), channel_id=1, source_target_pairs={{0,1},{1,4},{4,5},{5,8},{8,9},{9,12},{12,13},{2,3},{3,6},{6,7},{7,... | collective-permute-start | bytes 36872 | tf_op jit(solution)/shard_map/ppermute | solution.py:17
  6.5 1.3 %collective-permute-start.2 = (f32[3,4,1,256]{3,1,2,0:T(4,128)S(1)}, f32[3,4,1,256]{3,1,2,0:T(4,128)S(1)}, u32[]{:S(2)}, u32[]{:S(2)}) collective-permute-start(f32[3,4,1,256]{3,1,2,0:T(4,128)S(1)} %get-tuple-element.63), channel_id=1, source_target_pairs={{1,0},{4,1},{5,4},{8,5},{9,8},{12,9},{13,12},{3,2},{6,3},{7,6},{10... | collective-permute-start | bytes 36872 | tf_op jit(solution)/shard_map/ppermute | solution.py:18
  9.6 2.2 %collective-permute-done.2 = f32[3,4,1,256]{3,1,2,0:T(4,128)S(1)} collective-permute-done((f32[3,4,1,256]{3,1,2,0:T(4,128)S(1)}, f32[3,4,1,256]{3,1,2,0:T(4,128)S(1)}, u32[]{:S(2)}, u32[]{:S(2)}) %collective-permute-start.2) | collective-permute-done | bytes 12320 | tf_op jit(solution)/shard_map/ppermute | solution.py:18
  12.5 4.3 %collective-permute-start.3 = (f32[3,4,1,256]{3,1,2,0:T(4,128)S(1)}, f32[3,4,1,256]{3,1,2,0:T(4,128)S(1)}, u32[]{:S(2)}, u32[]{:S(2)}) collective-permute-start(f32[3,4,1,256]{3,1,2,0:T(4,128)S(1)} %get-tuple-element.60), channel_id=1, source_target_pairs={{0,1},{1,4},{4,5},{5,8},{8,9},{9,12},{12,13},{2,3},{3,6},{6,7},{7,... | collective-permute-start | bytes 36872 | tf_op jit(solution)/shard_map/ppermute | solution.py:17
  16.8 1.3 %collective-permute-start.4 = (f32[3,4,1,256]{3,1,2,0:T(4,128)S(1)}, f32[3,4,1,256]{3,1,2,0:T(4,128)S(1)}, u32[]{:S(2)}, u32[]{:S(2)}) collective-permute-start(f32[3,4,1,256]{3,1,2,0:T(4,128)S(1)} %get-tuple-element.61), channel_id=1, source_target_pairs={{1,0},{4,1},{5,4},{8,5},{9,8},{12,9},{13,12},{3,2},{6,3},{7,6},{10... | collective-permute-start | bytes 36872 | tf_op jit(solution)/shard_map/ppermute | solution.py:18
  18.7 1.8 %reshape.56 = f32[2,1,8192]{2,1,0:T(1,128)} reshape(f32[256,2,4,8]{3,2,1,0:T(4,128)S(1)} %bitcast.80) | data formatting | bytes 131072
  20.5 3.4 %all-to-all-start = ((f32[2,1,8192]{2,1,0:T(1,128)}), f32[2,1,8192]{2,1,0:T(1,128)S(1)}, u32[]{:S(2)}, u32[]{:S(2)}) async-start(f32[2,1,8192]{2,1,0:T(1,128)} %reshape.56), calls=%async_computation | async-start | bytes 131072 | tf_op jit(solution)/shard_map/all_to_all | solution.py:142
  24.1 4.1 %all-to-all-done = f32[2,1,8192]{2,1,0:T(1,128)S(1)} async-done(((f32[2,1,8192]{2,1,0:T(1,128)}), f32[2,1,8192]{2,1,0:T(1,128)S(1)}, u32[]{:S(2)}, u32[]{:S(2)}) %all-to-all-start) | async-done | bytes 65568 | tf_op jit(solution)/shard_map/all_to_all | solution.py:142
  29.6 1.3 %reshape.57 = f32[256,2,4,8]{3,2,1,0:T(4,128)S(1)} reshape(f32[2,8192]{1,0:T(2,128)S(1)} %reduce) | data formatting | bytes 131072
  31.4 2.0 %collective-permute-start.5 = (f32[26,8,1,128]{3,2,1,0:T(1,128)S(1)}, f32[26,8,1,128]{3,2,1,0:T(1,128)S(1)}, u32[]{:S(2)}, u32[]{:S(2)}) collective-permute-start(f32[26,8,1,128]{3,2,1,0:T(1,128)S(1)} %get-tuple-element.40), channel_id=1, source_target_pairs={{0,1},{1,4},{4,5},{5,8},{8,9},{9,12},{12,13},{2,3},{3,6},{6,7},{7,... | collective-permute-start | bytes 319496 | tf_op jit(solution)/shard_map/ppermute | solution.py:17
  33.4 1.3 %collective-permute-start.6 = (f32[26,8,1,128]{3,2,1,0:T(1,128)S(1)}, f32[26,8,1,128]{3,2,1,0:T(1,128)S(1)}, u32[]{:S(2)}, u32[]{:S(2)}) collective-permute-start(f32[26,8,1,128]{3,2,1,0:T(1,128)S(1)} %get-tuple-element.41), channel_id=1, source_target_pairs={{1,0},{4,1},{5,4},{8,5},{9,8},{12,9},{13,12},{3,2},{6,3},{7,6},{10... | collective-permute-start | bytes 319496 | tf_op jit(solution)/shard_map/ppermute | solution.py:18
  34.8 3.8 %collective-permute-done.6 = f32[26,8,1,128]{3,2,1,0:T(1,128)S(1)} collective-permute-done((f32[26,8,1,128]{3,2,1,0:T(1,128)S(1)}, f32[26,8,1,128]{3,2,1,0:T(1,128)S(1)}, u32[]{:S(2)}, u32[]{:S(2)}) %collective-permute-start.6) | collective-permute-done | bytes 106528 | tf_op jit(solution)/shard_map/ppermute | solution.py:18
  39.0 1.8 %fusion.102 = (f32[26,8,10,1]{3,2,1,0:T(8,128)}, f32[26,8,10,1]{3,2,1,0:T(8,128)S(1)}) fusion(f32[26,8,10,128]{3,2,1,0:T(8,128)S(1)} %pad_maximum_fusion), kind=kLoop, calls=%fused_computation.213 | loop fusion | bytes 33280 | tf_op jit(solution)/shard_map/slice | solution.py:15
  40.8 2.2 %copy.146 = f32[26,8,10,1]{0,1,3,2:T(8,128)S(1)} copy(f32[26,8,10,1]{3,2,1,0:T(8,128)} %get-tuple-element.36) | data formatting | bytes 16640 | tf_op jit(solution)/shard_map/slice | solution.py:15
  43.0 0.9 copy.147
  43.9 1.3 %collective-permute-start.8 = (f32[26,8,10,1]{0,1,3,2:T(8,128)S(1)}, f32[26,8,10,1]{0,1,3,2:T(8,128)S(1)}, u32[]{:S(2)}, u32[]{:S(2)}) collective-permute-start(f32[26,8,10,1]{0,1,3,2:T(8,128)S(1)} %copy.147), channel_id=1, source_target_pairs={{2,0},{3,1},{6,4},{7,5},{10,8},{11,9},{14,12},{15,13},{18,16},{19,... | collective-permute-start | bytes 24968 | tf_op jit(solution)/shard_map/ppermute | solution.py:18
  45.2 4.5 %collective-permute-start.7 = (f32[26,8,10,1]{0,1,3,2:T(8,128)S(1)}, f32[26,8,10,1]{0,1,3,2:T(8,128)S(1)}, u32[]{:S(2)}, u32[]{:S(2)}) collective-permute-start(f32[26,8,10,1]{0,1,3,2:T(8,128)S(1)} %copy.146), channel_id=1, source_target_pairs={{0,2},{1,3},{4,6},{5,7},{8,10},{9,11},{12,14},{13,15},{16,18},{17,... | collective-permute-start | bytes 24968 | tf_op jit(solution)/shard_map/ppermute | solution.py:17
  51.4 1.6 %copy.148 = f32[26,8,10,1]{3,2,1,0:T(8,128)S(1)} copy(f32[26,8,10,1]{0,1,3,2:T(8,128)S(1)} %collective-permute-done.7) | data formatting | bytes 16640 | tf_op jit(solution)/shard_map/ppermute | solution.py:17
  53.0 2.6 %copy.149 = f32[26,8,10,1]{3,2,1,0:T(8,128)} copy(f32[26,8,10,1]{0,1,3,2:T(8,128)S(1)} %collective-permute-done.8) | data formatting | bytes 16640 | tf_op jit(solution)/shard_map/ppermute | solution.py:18
  55.6 1.2 %maximum_bitcast_fusion.1 = (f32[8,10,130]{2,1,0:T(8,128)S(1)}, f32[8,10,130]{2,1,0:T(8,128)S(1)}) fusion(f32[26,8,10,1]{3,2,1,0:T(8,128)} %copy.149, f32[26,8,10,1]{3,2,1,0:T(8,128)S(1)} %copy.148, f32[26,8,1,128]{3,2,1,0:T(1,128)S(1)} %collective-permute-done.6, f32[26,8,1,128]{3,2,1,0:T(1,128)S(1)} %collective-permute-done.5, ...), kind=kLoop, calls=%fused_computation.80 | loop fusion | flops 104000 | bytes 1164800 | tf_op jit(solution)/shard_map/squeeze | solution.py:75
  57.1 1.2 fusion.10
  59.8 3.6 %all-to-all-start.1 = ((f32[8,8,128]{2,1,0:T(8,128)}), f32[8,8,128]{2,1,0:T(8,128)S(1)}, u32[]{:S(2)}, u32[]{:S(2)}) async-start(f32[8,8,128]{2,1,0:T(8,128)} %get-tuple-element.67), calls=%async_computation.1 | async-start | bytes 65536 | tf_op jit(solution)/shard_map/all_to_all | solution.py:150
  63.4 1.2 %fusion.22 = f32[8,8,128,24]{2,3,1,0:T(8,128)S(1)} fusion(f32[24,8,8,128]{3,2,1,0:T(8,128)S(1)} %fusion.17, f32[24,24]{1,0:T(8,128)S(1)} %copy-done), kind=kOutput, calls=%fused_computation.56 | convolution fusion | flops 56623104 | bytes 1575168 | tf_op jit(solution)/shard_map/ab,bzyx->azyx/dot_general | solution.py:96
  64.6 2.8 %all-to-all-done.1 = f32[8,8,128]{2,1,0:T(8,128)S(1)} async-done(((f32[8,8,128]{2,1,0:T(8,128)}), f32[8,8,128]{2,1,0:T(8,128)S(1)}, u32[]{:S(2)}, u32[]{:S(2)}) %all-to-all-start.1) | async-done | bytes 32800 | tf_op jit(solution)/shard_map/all_to_all | solution.py:150
  67.6 0.9 fusion.46
  69.0 1.8 %reshape.58 = f32[2,1,8192]{2,1,0:T(1,128)} reshape(f32[256,2,4,8]{3,2,1,0:T(4,128)S(1)} %bitcast.82) | data formatting | bytes 131072
  70.8 3.3 %all-to-all-start.2 = ((f32[2,1,8192]{2,1,0:T(1,128)}), f32[2,1,8192]{2,1,0:T(1,128)S(1)}, u32[]{:S(2)}, u32[]{:S(2)}) async-start(f32[2,1,8192]{2,1,0:T(1,128)} %reshape.58), calls=%async_computation.2 | async-start | bytes 131072 | tf_op jit(solution)/shard_map/all_to_all | solution.py:142
  74.1 1.0 fusion.19
  75.1 3.4 %all-to-all-done.2 = f32[2,1,8192]{2,1,0:T(1,128)S(1)} async-done(((f32[2,1,8192]{2,1,0:T(1,128)}), f32[2,1,8192]{2,1,0:T(1,128)S(1)}, u32[]{:S(2)}, u32[]{:S(2)}) %all-to-all-start.2) | async-done | bytes 65568 | tf_op jit(solution)/shard_map/all_to_all | solution.py:142
  79.3 1.3 %reshape.59 = f32[256,2,4,8]{3,2,1,0:T(4,128)S(1)} reshape(f32[2,8192]{1,0:T(2,128)S(1)} %reduce.1) | data formatting | bytes 131072
  81.1 2.0 %collective-permute-start.9 = (f32[26,8,1,128]{3,2,1,0:T(1,128)S(1)}, f32[26,8,1,128]{3,2,1,0:T(1,128)S(1)}, u32[]{:S(2)}, u32[]{:S(2)}) collective-permute-start(f32[26,8,1,128]{3,2,1,0:T(1,128)S(1)} %get-tuple-element.38), channel_id=1, source_target_pairs={{0,1},{1,4},{4,5},{5,8},{8,9},{9,12},{12,13},{2,3},{3,6},{6,7},{7,... | collective-permute-start | bytes 319496 | tf_op jit(solution)/shard_map/ppermute | solution.py:17
  83.2 1.3 %collective-permute-start.10 = (f32[26,8,1,128]{3,2,1,0:T(1,128)S(1)}, f32[26,8,1,128]{3,2,1,0:T(1,128)S(1)}, u32[]{:S(2)}, u32[]{:S(2)}) collective-permute-start(f32[26,8,1,128]{3,2,1,0:T(1,128)S(1)} %get-tuple-element.39), channel_id=1, source_target_pairs={{1,0},{4,1},{5,4},{8,5},{9,8},{12,9},{13,12},{3,2},{6,3},{7,6},{10... | collective-permute-start | bytes 319496 | tf_op jit(solution)/shard_map/ppermute | solution.py:18
  84.5 4.2 %collective-permute-done.10 = f32[26,8,1,128]{3,2,1,0:T(1,128)S(1)} collective-permute-done((f32[26,8,1,128]{3,2,1,0:T(1,128)S(1)}, f32[26,8,1,128]{3,2,1,0:T(1,128)S(1)}, u32[]{:S(2)}, u32[]{:S(2)}) %collective-permute-start.10) | collective-permute-done | bytes 106528 | tf_op jit(solution)/shard_map/ppermute | solution.py:18
  89.0 1.8 %fusion.101 = (f32[26,8,10,1]{3,2,1,0:T(8,128)}, f32[26,8,10,1]{3,2,1,0:T(8,128)S(1)}) fusion(f32[26,8,10,128]{3,2,1,0:T(8,128)S(1)} %pad_maximum_fusion.1), kind=kLoop, calls=%fused_computation.212 | loop fusion | bytes 33280 | tf_op jit(solution)/shard_map/slice | solution.py:15
  90.8 2.2 %copy.157 = f32[26,8,10,1]{0,1,3,2:T(8,128)S(1)} copy(f32[26,8,10,1]{3,2,1,0:T(8,128)} %get-tuple-element.34) | data formatting | bytes 16640 | tf_op jit(solution)/shard_map/slice | solution.py:15
  93.0 1.9 %collective-permute-start.11 = (f32[26,8,10,1]{0,1,3,2:T(8,128)S(1)}, f32[26,8,10,1]{0,1,3,2:T(8,128)S(1)}, u32[]{:S(2)}, u32[]{:S(2)}) collective-permute-start(f32[26,8,10,1]{0,1,3,2:T(8,128)S(1)} %copy.157), channel_id=1, source_target_pairs={{0,2},{1,3},{4,6},{5,7},{8,10},{9,11},{12,14},{13,15},{16,18},{17,... | collective-permute-start | bytes 24968 | tf_op jit(solution)/shard_map/ppermute | solution.py:17
  95.0 0.9 copy.158
  95.9 1.5 %collective-permute-start.12 = (f32[26,8,10,1]{0,1,3,2:T(8,128)S(1)}, f32[26,8,10,1]{0,1,3,2:T(8,128)S(1)}, u32[]{:S(2)}, u32[]{:S(2)}) collective-permute-start(f32[26,8,10,1]{0,1,3,2:T(8,128)S(1)} %copy.158), channel_id=1, source_target_pairs={{2,0},{3,1},{6,4},{7,5},{10,8},{11,9},{14,12},{15,13},{18,16},{19,... | collective-permute-start | bytes 24968 | tf_op jit(solution)/shard_map/ppermute | solution.py:18
  99.3 1.6 %copy.159 = f32[26,8,10,1]{3,2,1,0:T(8,128)S(1)} copy(f32[26,8,10,1]{0,1,3,2:T(8,128)S(1)} %collective-permute-done.11) | data formatting | bytes 16640 | tf_op jit(solution)/shard_map/ppermute | solution.py:17
  100.9 0.9 collective-permute-done.12
  101.8 2.6 %copy.160 = f32[26,8,10,1]{3,2,1,0:T(8,128)} copy(f32[26,8,10,1]{0,1,3,2:T(8,128)S(1)} %collective-permute-done.12) | data formatting | bytes 16640 | tf_op jit(solution)/shard_map/ppermute | solution.py:18
  104.4 1.2 %maximum_bitcast_fusion = (f32[8,10,130]{2,1,0:T(8,128)S(1)}, f32[8,10,130]{2,1,0:T(8,128)S(1)}) fusion(f32[26,8,10,1]{3,2,1,0:T(8,128)} %copy.160, f32[26,8,10,1]{3,2,1,0:T(8,128)S(1)} %copy.159, f32[26,8,1,128]{3,2,1,0:T(1,128)S(1)} %collective-permute-done.10, f32[26,8,1,128]{3,2,1,0:T(1,128)S(1)} %collective-permute-done.9, ...), kind=kLoop, calls=%fused_computation.73 | loop fusion | flops 104000 | bytes 1164800 | tf_op jit(solution)/shard_map/squeeze | solution.py:75
  105.9 1.1 fusion.4
  107.8 1.2 %fusion.20 = f32[8,8,128,24]{2,3,1,0:T(8,128)S(1)} fusion(f32[24,8,8,128]{3,2,1,0:T(8,128)S(1)} %fusion.14, f32[24,24]{1,0:T(8,128)S(1)} %copy-done), kind=kOutput, calls=%fused_computation.53 | convolution fusion | flops 56623104 | bytes 1575168 | tf_op jit(solution)/shard_map/ab,bzyx->azyx/dot_general | solution.py:96
  109.7 3.3 %all-to-all-start.3 = ((f32[8,8,128]{2,1,0:T(8,128)}), f32[8,8,128]{2,1,0:T(8,128)S(1)}, u32[]{:S(2)}, u32[]{:S(2)}) async-start(f32[8,8,128]{2,1,0:T(8,128)} %get-tuple-element.65), calls=%async_computation.3 | async-start | bytes 65536 | tf_op jit(solution)/shard_map/all_to_all | solution.py:150
  113.0 1.1 fusion.18
  114.1 2.8 %all-to-all-done.3 = f32[8,8,128]{2,1,0:T(8,128)S(1)} async-done(((f32[8,8,128]{2,1,0:T(8,128)}), f32[8,8,128]{2,1,0:T(8,128)S(1)}, u32[]{:S(2)}, u32[]{:S(2)}) %all-to-all-start.3) | async-done | bytes 32800 | tf_op jit(solution)/shard_map/all_to_all | solution.py:150
  (90 shorter events, 16.7 us)
Async XLA Ops:
  0.6 62.7 %copy-start = (f32[24,24]{1,0:T(8,128)S(1)}, f32[24,24]{1,0:T(8,128)}, u32[]{:S(2)}) copy-start(f32[24,24]{1,0:T(8,128)} %param.13) | copy-start | bytes 6916
  0.6 11.6 %copy-start.12 = (f32[4,8,256]{2,1,0:T(8,128)S(1)}, f32[4,8,256]{2,1,0:T(8,128)}, u32[]{:S(2)}) copy-start(f32[4,8,256]{2,1,0:T(8,128)} %param.10) | copy-start | bytes 98308
  1.4 6.5 %collective-permute-start = (s32[1,256]{1,0:T(1,128)S(1)}, s32[1,256]{1,0:T(1,128)S(1)}, u32[]{:S(2)}, u32[]{:S(2)}) collective-permute-start(s32[1,256]{1,0:T(1,128)S(1)} %slice.289), channel_id=1, source_target_pairs={{1,0},{4,1},{5,4},{8,5},{9,8},{12,9},{13,12},{3,2},{6,3},{7,6},{10... | collective-permute-start | bytes 3080 | tf_op jit(solution)/shard_map/ppermute | solution.py:26
  3.5 6.1 %collective-permute-start.1 = (f32[3,4,1,256]{3,1,2,0:T(4,128)S(1)}, f32[3,4,1,256]{3,1,2,0:T(4,128)S(1)}, u32[]{:S(2)}, u32[]{:S(2)}) collective-permute-start(f32[3,4,1,256]{3,1,2,0:T(4,128)S(1)} %get-tuple-element.62), channel_id=1, source_target_pairs={{0,1},{1,4},{4,5},{5,8},{8,9},{9,12},{12,13},{2,3},{3,6},{6,7},{7,... | collective-permute-start | bytes 36872 | tf_op jit(solution)/shard_map/ppermute | solution.py:17
  6.5 5.2 %collective-permute-start.2 = (f32[3,4,1,256]{3,1,2,0:T(4,128)S(1)}, f32[3,4,1,256]{3,1,2,0:T(4,128)S(1)}, u32[]{:S(2)}, u32[]{:S(2)}) collective-permute-start(f32[3,4,1,256]{3,1,2,0:T(4,128)S(1)} %get-tuple-element.63), channel_id=1, source_target_pairs={{1,0},{4,1},{5,4},{8,5},{9,8},{12,9},{13,12},{3,2},{6,3},{7,6},{10... | collective-permute-start | bytes 36872 | tf_op jit(solution)/shard_map/ppermute | solution.py:18
  12.5 11.4 %collective-permute-start.3 = (f32[3,4,1,256]{3,1,2,0:T(4,128)S(1)}, f32[3,4,1,256]{3,1,2,0:T(4,128)S(1)}, u32[]{:S(2)}, u32[]{:S(2)}) collective-permute-start(f32[3,4,1,256]{3,1,2,0:T(4,128)S(1)} %get-tuple-element.60), channel_id=1, source_target_pairs={{0,1},{1,4},{4,5},{5,8},{8,9},{9,12},{12,13},{2,3},{3,6},{6,7},{7,... | collective-permute-start | bytes 36872 | tf_op jit(solution)/shard_map/ppermute | solution.py:17
  16.8 7.1 %collective-permute-start.4 = (f32[3,4,1,256]{3,1,2,0:T(4,128)S(1)}, f32[3,4,1,256]{3,1,2,0:T(4,128)S(1)}, u32[]{:S(2)}, u32[]{:S(2)}) collective-permute-start(f32[3,4,1,256]{3,1,2,0:T(4,128)S(1)} %get-tuple-element.61), channel_id=1, source_target_pairs={{1,0},{4,1},{5,4},{8,5},{9,8},{12,9},{13,12},{3,2},{6,3},{7,6},{10... | collective-permute-start | bytes 36872 | tf_op jit(solution)/shard_map/ppermute | solution.py:18
  20.5 10.8 %copy-start.1 = (f32[24,8,8,128]{3,2,1,0:T(8,128)S(1)}, f32[24,8,8,128]{3,2,1,0:T(8,128)}, u32[]{:S(2)}) copy-start(f32[24,8,8,128]{3,2,1,0:T(8,128)} %param.11) | copy-start | bytes 2359300
  20.5 7.7 %all-to-all-start = ((f32[2,1,8192]{2,1,0:T(1,128)}), f32[2,1,8192]{2,1,0:T(1,128)S(1)}, u32[]{:S(2)}, u32[]{:S(2)}) async-start(f32[2,1,8192]{2,1,0:T(1,128)} %reshape.56), calls=%async_computation | async-start | bytes 131072 | tf_op jit(solution)/shard_map/all_to_all | solution.py:142
  31.4 3.4 %collective-permute-start.5 = (f32[26,8,1,128]{3,2,1,0:T(1,128)S(1)}, f32[26,8,1,128]{3,2,1,0:T(1,128)S(1)}, u32[]{:S(2)}, u32[]{:S(2)}) collective-permute-start(f32[26,8,1,128]{3,2,1,0:T(1,128)S(1)} %get-tuple-element.40), channel_id=1, source_target_pairs={{0,1},{1,4},{4,5},{5,8},{8,9},{9,12},{12,13},{2,3},{3,6},{6,7},{7,... | collective-permute-start | bytes 319496 | tf_op jit(solution)/shard_map/ppermute | solution.py:17
  33.4 5.2 %collective-permute-start.6 = (f32[26,8,1,128]{3,2,1,0:T(1,128)S(1)}, f32[26,8,1,128]{3,2,1,0:T(1,128)S(1)}, u32[]{:S(2)}, u32[]{:S(2)}) collective-permute-start(f32[26,8,1,128]{3,2,1,0:T(1,128)S(1)} %get-tuple-element.41), channel_id=1, source_target_pairs={{1,0},{4,1},{5,4},{8,5},{9,8},{12,9},{13,12},{3,2},{6,3},{7,6},{10... | collective-permute-start | bytes 319496 | tf_op jit(solution)/shard_map/ppermute | solution.py:18
  34.8 15.0 %copy-start.4 = (f32[4,10,258]{2,0,1:T(4,128)}, f32[4,10,258]{2,0,1:T(4,128)S(1)}, u32[]{:S(2)}) copy-start(f32[4,10,258]{2,0,1:T(4,128)S(1)} %get-tuple-element.43) | copy-start | bytes 123844
  43.9 9.1 %collective-permute-start.8 = (f32[26,8,10,1]{0,1,3,2:T(8,128)S(1)}, f32[26,8,10,1]{0,1,3,2:T(8,128)S(1)}, u32[]{:S(2)}, u32[]{:S(2)}) collective-permute-start(f32[26,8,10,1]{0,1,3,2:T(8,128)S(1)} %copy.147), channel_id=1, source_target_pairs={{2,0},{3,1},{6,4},{7,5},{10,8},{11,9},{14,12},{15,13},{18,16},{19,... | collective-permute-start | bytes 24968 | tf_op jit(solution)/shard_map/ppermute | solution.py:18
  45.2 6.2 %collective-permute-start.7 = (f32[26,8,10,1]{0,1,3,2:T(8,128)S(1)}, f32[26,8,10,1]{0,1,3,2:T(8,128)S(1)}, u32[]{:S(2)}, u32[]{:S(2)}) collective-permute-start(f32[26,8,10,1]{0,1,3,2:T(8,128)S(1)} %copy.146), channel_id=1, source_target_pairs={{0,2},{1,3},{4,6},{5,7},{8,10},{9,11},{12,14},{13,15},{16,18},{17,... | collective-permute-start | bytes 24968 | tf_op jit(solution)/shard_map/ppermute | solution.py:17
  55.6 1.5 %copy-start.2 = (f32[26,8,10,1]{3,2,1,0:T(8,128)S(1)}, f32[26,8,10,1]{3,2,1,0:T(8,128)}, u32[]{:S(2)}) copy-start(f32[26,8,10,1]{3,2,1,0:T(8,128)} %copy.149) | copy-start | bytes 24964
  59.1 8.5 %copy-start.5 = (f32[4,10,258]{2,0,1:T(4,128)S(1)}, f32[4,10,258]{2,0,1:T(4,128)}, u32[]{:S(2)}) copy-start(f32[4,10,258]{2,0,1:T(4,128)} %copy-done.4) | copy-start | bytes 123844
  59.1 9.3 %copy-start.9 = (f32[4,8,256]{2,0,1:T(4,128)S(1)}, f32[4,8,256]{2,0,1:T(4,128)}, u32[]{:S(2)}) copy-start(f32[4,8,256]{2,0,1:T(4,128)} %fusion.59) | copy-start | bytes 98308
  59.8 7.7 %all-to-all-start.1 = ((f32[8,8,128]{2,1,0:T(8,128)}), f32[8,8,128]{2,1,0:T(8,128)S(1)}, u32[]{:S(2)}, u32[]{:S(2)}) async-start(f32[8,8,128]{2,1,0:T(8,128)} %get-tuple-element.67), calls=%async_computation.1 | async-start | bytes 65536 | tf_op jit(solution)/shard_map/all_to_all | solution.py:150
  68.4 5.6 %copy-start.7 = (f32[4,8,256]{2,0,1:T(4,128)}, f32[4,8,256]{2,0,1:T(4,128)S(1)}, u32[]{:S(2)}) copy-start(f32[4,8,256]{2,0,1:T(4,128)S(1)} %get-tuple-element.57) | copy-start | bytes 98308
  70.8 7.7 %all-to-all-start.2 = ((f32[2,1,8192]{2,1,0:T(1,128)}), f32[2,1,8192]{2,1,0:T(1,128)S(1)}, u32[]{:S(2)}, u32[]{:S(2)}) async-start(f32[2,1,8192]{2,1,0:T(1,128)} %reshape.58), calls=%async_computation.2 | async-start | bytes 131072 | tf_op jit(solution)/shard_map/all_to_all | solution.py:142
  81.1 3.3 %collective-permute-start.9 = (f32[26,8,1,128]{3,2,1,0:T(1,128)S(1)}, f32[26,8,1,128]{3,2,1,0:T(1,128)S(1)}, u32[]{:S(2)}, u32[]{:S(2)}) collective-permute-start(f32[26,8,1,128]{3,2,1,0:T(1,128)S(1)} %get-tuple-element.38), channel_id=1, source_target_pairs={{0,1},{1,4},{4,5},{5,8},{8,9},{9,12},{12,13},{2,3},{3,6},{6,7},{7,... | collective-permute-start | bytes 319496 | tf_op jit(solution)/shard_map/ppermute | solution.py:17
  83.2 5.5 %collective-permute-start.10 = (f32[26,8,1,128]{3,2,1,0:T(1,128)S(1)}, f32[26,8,1,128]{3,2,1,0:T(1,128)S(1)}, u32[]{:S(2)}, u32[]{:S(2)}) collective-permute-start(f32[26,8,1,128]{3,2,1,0:T(1,128)S(1)} %get-tuple-element.39), channel_id=1, source_target_pairs={{1,0},{4,1},{5,4},{8,5},{9,8},{12,9},{13,12},{3,2},{6,3},{7,6},{10... | collective-permute-start | bytes 319496 | tf_op jit(solution)/shard_map/ppermute | solution.py:18
  90.8 6.6 %copy-start.10 = (f32[4,8,256]{2,0,1:T(4,128)S(1)}, f32[4,8,256]{2,0,1:T(4,128)}, u32[]{:S(2)}) copy-start(f32[4,8,256]{2,0,1:T(4,128)} %fusion.59) | copy-start | bytes 98308
  90.8 7.2 %copy-start.8 = (f32[4,8,256]{2,0,1:T(4,128)S(1)}, f32[4,8,256]{2,0,1:T(4,128)}, u32[]{:S(2)}) copy-start(f32[4,8,256]{2,0,1:T(4,128)} %copy-done.7) | copy-start | bytes 98308
  90.8 7.8 %copy-start.11 = (f32[4,8,256]{2,0,1:T(4,128)S(1)}, f32[4,8,256]{2,0,1:T(4,128)}, u32[]{:S(2)}) copy-start(f32[4,8,256]{2,0,1:T(4,128)} %get-tuple-element.56) | copy-start | bytes 98308
  93.0 6.3 %collective-permute-start.11 = (f32[26,8,10,1]{0,1,3,2:T(8,128)S(1)}, f32[26,8,10,1]{0,1,3,2:T(8,128)S(1)}, u32[]{:S(2)}, u32[]{:S(2)}) collective-permute-start(f32[26,8,10,1]{0,1,3,2:T(8,128)S(1)} %copy.157), channel_id=1, source_target_pairs={{0,2},{1,3},{4,6},{5,7},{8,10},{9,11},{12,14},{13,15},{16,18},{17,... | collective-permute-start | bytes 24968 | tf_op jit(solution)/shard_map/ppermute | solution.py:17
  95.9 5.9 %collective-permute-start.12 = (f32[26,8,10,1]{0,1,3,2:T(8,128)S(1)}, f32[26,8,10,1]{0,1,3,2:T(8,128)S(1)}, u32[]{:S(2)}, u32[]{:S(2)}) collective-permute-start(f32[26,8,10,1]{0,1,3,2:T(8,128)S(1)} %copy.158), channel_id=1, source_target_pairs={{2,0},{3,1},{6,4},{7,5},{10,8},{11,9},{14,12},{15,13},{18,16},{19,... | collective-permute-start | bytes 24968 | tf_op jit(solution)/shard_map/ppermute | solution.py:18
  104.4 1.5 %copy-start.3 = (f32[26,8,10,1]{3,2,1,0:T(8,128)S(1)}, f32[26,8,10,1]{3,2,1,0:T(8,128)}, u32[]{:S(2)}) copy-start(f32[26,8,10,1]{3,2,1,0:T(8,128)} %copy.160) | copy-start | bytes 24964
  107.8 5.2 %copy-start.6 = (f32[8,8,128]{2,1,0:T(8,128)S(1)}, f32[8,8,128]{2,1,0:T(8,128)}, u32[]{:S(2)}) copy-start(f32[8,8,128]{2,1,0:T(8,128)} %fusion.41) | copy-start | bytes 98308
  109.7 7.2 %all-to-all-start.3 = ((f32[8,8,128]{2,1,0:T(8,128)}), f32[8,8,128]{2,1,0:T(8,128)S(1)}, u32[]{:S(2)}, u32[]{:S(2)}) async-start(f32[8,8,128]{2,1,0:T(8,128)} %get-tuple-element.65), calls=%async_computation.3 | async-start | bytes 65536 | tf_op jit(solution)/shard_map/all_to_all | solution.py:150
where the time goes:
time: 120 us; the launch traced here: 118 us
  starting transfers between devices  40.7 us (34%)
  local copies, waits for them, and re-layouts  30.7 us (26%)
  waiting for transfers between devices  25.1 us (21%)
  other arithmetic  17.3 us (14%)
  matrix products  2.5 us (2%)
  between operations  1.25 us (1%)
    ppermute x6, starting transfers between devices, padded(): before = lax.ppermute(last, axis, up)  17.9 us
    ppermute x6, waiting for transfers between devices, padded(): after = lax.ppermute(leading, axis, down)  11.1 us
    unnamed x33, local copies, waits for them, and re-layouts  8.39 us
    slice x5, local copies, waits for them, and re-layouts, padded(): last = lax.slice_in_dim(shard, length - width, length, axis=dim)  8.04 us
    ppermute x6, starting transfers between devices, padded(): after = lax.ppermute(leading, axis, down)  7.96 us
    all_to_all x2, waiting for transfers between devices, shards(): lax.all_to_all(jnp.stack([eastward_current, poleward_current]), 'lon', sp...  7.52 us
    all_to_all x2, starting transfers between devices, shards(): lax.all_to_all(heat_tile, 'lon', split_axis=0, concat_axis=2, tiled=True)  6.85 us
    all_to_all x2, starting transfers between devices, shards(): lax.all_to_all(jnp.stack([eastward_current, poleward_current]), 'lon', sp...  6.73 us
  transfers between devices with their start and end apart: 17, of which 9 were waited for; matrix products, arithmetic and copies ran while one was open for 13% of the time, Pallas kernels for 0%

commit v1 on v0

v1 whole, which is shorter than its diff:
```python
import functools

import jax
import jax.numpy as jnp
from jax import lax
from jax.experimental import pallas as pl
from jax.experimental.pallas import tpu as pltpu
from jax.sharding import PartitionSpec as P

ROWS = 8
LANES = 128
PAD = 4
EXT = ROWS + 2 * PAD
F32 = jnp.float32


def east(q):
    lane = lax.broadcasted_iota(jnp.int32, q.shape, q.ndim - 1)
    return jnp.where(lane < q.shape[-1] - 1, pltpu.roll(q, q.shape[-1] - 1, q.ndim - 1), 0.0)


def west(q):
    lane = lax.broadcasted_iota(jnp.int32, q.shape, q.ndim - 1)
    return jnp.where(lane > 0, pltpu.roll(q, 1, q.ndim - 1), 0.0)


def north(q):
    return pltpu.roll(q, q.shape[-2] - 1, q.ndim - 2)


def south(q):
    return pltpu.roll(q, 1, q.ndim - 2)


def lap(q):
    return east(q) + west(q) + north(q) + south(q) - 4.0 * q


def kernel(
    sizes,
    u_in, v_in, t_in, h_in, c_in, n_in, r_in,
    u_out, v_out, t_out, h_out, c_out,
    pk_n, pk_s, rc_n, rc_s, cnt_n, cnt_s, ext, ext_n, t_base, wet_strip,
    c_mid, row_lo, row_hi, col_ed, got_n, got_s, got_w, got_e,
    f_send, f_recv, h_send, h_recv,
    d_ssem, d_rsem, c0_ssem, c0_rsem, c1_ssem, c1_rsem, f_ssem, f_rsem, h_ssem, h_rsem,
):
    tracers, depth, share, nlon, nrole, nstrip = sizes
    width = nlon * LANES
    s = lax.axis_index("lat") * nrole + lax.axis_index("role")
    col = lax.axis_index("lon")
    has_n, has_s = s < nstrip - 1, s > 0
    has_e, has_w = col < nlon - 1, col > 0
    sn, ss = lax.rem(s + 1, nstrip), lax.rem(s + nstrip - 1, nstrip)
    dev_n = {"lat": sn // nrole, "role": lax.rem(sn, nrole)}
    dev_s = {"lat": ss // nrole, "role": lax.rem(ss, nrole)}
    dev_e = {"lon": lax.rem(col + 1, nlon)}
    dev_w = {"lon": lax.rem(col + nlon - 1, nlon)}

    barrier = pltpu.get_barrier_semaphore()

    def greet(dev):
        pl.semaphore_signal(barrier, inc=1, device_id=dev, device_id_type=pl.DeviceIdType.MESH)

    pl.when(has_n)(lambda: greet(dev_n))
    pl.when(has_s)(lambda: greet(dev_s))
    for d in range(1, nlon):
        greet({"lon": lax.rem(col + d, nlon)})

    def copy(src, dst, ssem, rsem, dev):
        return pltpu.make_async_remote_copy(
            src_ref=src, dst_ref=dst, send_sem=ssem, recv_sem=rsem,
            device_id=dev, device_id_type=pl.DeviceIdType.MESH,
        )

    def start(copies):
        for c, send, _ in copies:
            pl.when(send)(c.start)

    def wait_recv(copies):
        for c, _, recv in copies:
            pl.when(recv)(c.wait_recv)

    def wait_send(copies):
        for c, send, _ in copies:
            pl.when(send)(c.wait_send)

    pk_n[:, 0:3, :] = v_in[:, 5:8, :]
    pk_n[:, 3:5, :] = u_in[:, 6:8, :]
    pk_n[:, 5:7, :] = t_in[:, 6:8, :]
    pk_n[:, 7:8, :] = h_in[:, 7:8, :]
    pk_s[:, 0:2, :] = u_in[:, 0:2, :]
    pk_s[:, 2:4, :] = v_in[:, 0:2, :]
    pk_s[:, 4:6, :] = t_in[:, 0:2, :]
    pk_s[:, 6:7, :] = h_in[:, 0:1, :]
    pk_s[:, 7:8, :] = h_in[:, 0:1, :]

    lane = lax.broadcasted_iota(jnp.int32, (ROWS, LANES), 1)
    row = lax.broadcasted_iota(jnp.int32, (ROWS, LANES), 0)

    def pack(m, k, x):
        row_lo[m, k] = x[:, 0, :]
        row_hi[m, k] = x[:, ROWS - 1, :]
        acc = x[0]
        for t in range(1, tracers):
            here = (lane == 2 * t - 1) | (lane == 2 * t)
            acc = jnp.where(here, pltpu.roll(x[t], 2 * t, 1), acc)
        col_ed[m, k] = acc

    for k in range(depth):
        pack(0, k, c_in[:, k])

    dyn = [
        (copy(pk_n, rc_s, d_ssem.at[0], d_rsem.at[0], dev_n), has_n, has_s),
        (copy(pk_s, rc_n, d_ssem.at[1], d_rsem.at[1], dev_s), has_s, has_n),
        (copy(n_in, cnt_s, d_ssem.at[2], d_rsem.at[2], dev_n), has_n, has_s),
        (copy(n_in, cnt_n, d_ssem.at[3], d_rsem.at[3], dev_s), has_s, has_n),
    ]
    first = [
        (copy(row_hi.at[0], got_s.at[0], c0_ssem.at[0], c0_rsem.at[0], dev_n), has_n, has_s),
        (copy(row_lo.at[0], got_n.at[0], c0_ssem.at[1], c0_rsem.at[1], dev_s), has_s, has_n),
        (copy(col_ed.at[0], got_w.at[0], c0_ssem.at[2], c0_rsem.at[2], dev_e), has_e, has_w),
        (copy(col_ed.at[0], got_e.at[0], c0_ssem.at[3], c0_rsem.at[3], dev_w), has_w, has_e),
    ]

    def second(k):
        return [
            (copy(row_hi.at[1, k], got_s.at[1, k], c1_ssem.at[0, k], c1_rsem.at[0, k], dev_n), has_n, has_s),
            (copy(row_lo.at[1, k], got_n.at[1, k], c1_ssem.at[1, k], c1_rsem.at[1, k], dev_s), has_s, has_n),
            (copy(col_ed.at[1, k], got_w.at[1, k], c1_ssem.at[2, k], c1_rsem.at[2, k], dev_e), has_e, has_w),
            (copy(col_ed.at[1, k], got_e.at[1, k], c1_ssem.at[3, k], c1_rsem.at[3, k], dev_w), has_w, has_e),
        ]

    def faces(m):
        out = []
        for d in range(1, nlon):
            p = lax.rem(col + d, nlon)
            out.append(copy(f_send.at[m, p], f_recv.at[m, col], f_ssem.at[m, d], f_rsem.at[m, d], {"lon": p}))
        return out

    def heats(m):
        out = []
        for d in range(1, nlon):
            p = lax.rem(col + d, nlon)
            out.append(copy(h_send.at[m, p], h_recv.at[m, col], h_ssem.at[m, d], h_rsem.at[m, d], {"lon": p}))
        return out

    pl.semaphore_wait(barrier, nlon - 1 + jnp.minimum(s, 1) + jnp.minimum(nstrip - 1 - s, 1))
    start(dyn)
    start(first)

    @pl.when(jnp.logical_not(has_s))
    def _():
        rc_s[...] = jnp.zeros_like(rc_s)
        cnt_s[...] = jnp.zeros_like(cnt_s)
        got_s[...] = jnp.zeros_like(got_s)

    @pl.when(jnp.logical_not(has_n))
    def _():
        rc_n[...] = jnp.zeros_like(rc_n)
        cnt_n[...] = jnp.zeros_like(cnt_n)
        got_n[...] = jnp.zeros_like(got_n)

    @pl.when(jnp.logical_not(has_w))
    def _():
        got_w[...] = jnp.zeros_like(got_w)

    @pl.when(jnp.logical_not(has_e))
    def _():
        got_e[...] = jnp.zeros_like(got_e)

    wide = tracers * ROWS
    spread = (
        lax.broadcasted_iota(jnp.int32, (wide, tracers), 0) // ROWS
        == lax.broadcasted_iota(jnp.int32, (wide, tracers), 1)
    ).astype(F32)
    gather = (
        lax.broadcasted_iota(jnp.int32, (tracers, wide), 1) // ROWS
        == lax.broadcasted_iota(jnp.int32, (tracers, wide), 0)
    ).astype(F32)
    exact = lax.Precision.HIGHEST
    rates = jnp.dot(
        spread, jnp.dot(r_in[...], gather, precision=exact, preferred_element_type=F32),
        precision=exact, preferred_element_type=F32,
    )
    same_row = (
        lax.broadcasted_iota(jnp.int32, (wide, wide), 0) % ROWS
        == lax.broadcasted_iota(jnp.int32, (wide, wide), 1) % ROWS
    )
    rates = jnp.where(same_row, rates, 0.0)
    rates_hi = rates.astype(jnp.bfloat16)
    rates_lo = (rates - rates_hi.astype(F32)).astype(jnp.bfloat16)

    zero = jnp.zeros((share, PAD, width), F32)
    for f in range(4):
        ext[f, :, 0:PAD, :] = zero
        ext[f, :, PAD + ROWS :, :] = zero
    ext_n[0:PAD, :] = jnp.zeros((PAD, width), jnp.int32)
    ext_n[PAD + ROWS :, :] = jnp.zeros((PAD, width), jnp.int32)
    for f, ref in enumerate((u_in, v_in, t_in, h_in)):
        ext[f, :, PAD : PAD + ROWS, :] = ref[...]
    ext_n[PAD : PAD + ROWS, :] = n_in[...]

    wait_recv(dyn)
    ext[0, :, 2:4, :] = rc_s[:, 3:5, :]
    ext[1, :, 1:4, :] = rc_s[:, 0:3, :]
    ext[2, :, 2:4, :] = rc_s[:, 5:7, :]
    ext[3, :, 3:4, :] = rc_s[:, 7:8, :]
    ext[0, :, 12:14, :] = rc_n[:, 0:2, :]
    ext[1, :, 12:14, :] = rc_n[:, 2:4, :]
    ext[2, :, 12:14, :] = rc_n[:, 4:6, :]
    ext[3, :, 12:13, :] = rc_n[:, 6:7, :]
    ext_n[2:4, :] = cnt_s[6:8, :]
    ext_n[12:14, :] = cnt_n[0:2, :]

    shape = (share, EXT, width)
    level = col * share + lax.broadcasted_iota(jnp.int32, shape, 0)
    wet = (level < ext_n[...][None]).astype(F32)
    wet_u = wet * east(wet)
    wet_v = wet * north(wet)
    spot = (s * ROWS - PAD + lax.broadcasted_iota(jnp.int32, shape, 1)).astype(F32)
    fcor = 0.3 * (2.0 * (spot + 0.5) / (nstrip * ROWS) - 1.0)

    def advance(u, v, t):
        new_u = wet_u * (u + 0.1 * lap(u) + fcor * v - 0.2 * (east(t) - t))
        new_v = wet_v * (v + 0.1 * lap(v) - fcor * u - 0.2 * (north(t) - t))
        return new_u, new_v

    def publish(m, u, v):
        for p in range(nlon):
            lo = p * LANES
            cols = slice(lo, lo + LANES)
            v_edge = jnp.zeros((ROWS, LANES), F32)
            u_edge = jnp.zeros((ROWS, LANES), F32)
            for l in range(share):
                f_send[m, p, l] = u[l, PAD : PAD + ROWS, cols]
                f_send[m, p, share + l] = v[l, PAD : PAD + ROWS, cols]
                v_edge = jnp.where(row == l, v[l, PAD - 1 : PAD, cols], v_edge)
                if p:
                    u_edge = jnp.where(lane == l, u[l, PAD : PAD + ROWS, lo - 1 : lo], u_edge)
            f_send[m, p, 2 * share] = v_edge
            f_send[m, p, 2 * share + 1] = u_edge
        for c in faces(m):
            c.start()
        f_recv[m, col] = f_send[m, col]

    u0, v0, t0 = ext[0], ext[1], ext[2]
    u1, v1 = advance(u0, v0, t0)
    publish(0, u1, v1)
    t1 = wet * (t0 + 0.1 * lap(t0) + 0.5 * ext[3])
    u2, v2 = advance(u1, v1, t1)
    publish(1, u2, v2)
    u_out[...] = u2[:, PAD : PAD + ROWS, :]
    v_out[...] = v2[:, PAD : PAD + ROWS, :]
    t_base[...] = (wet * (t1 + 0.1 * lap(t1)))[:, PAD : PAD + ROWS, :]
    wet_strip[...] = wet[:, PAD : PAD + ROWS, :]

    depth_here = n_in[:, pl.ds(pl.multiple_of(col * LANES, LANES), LANES)]

    def tile_step(m, source, target):
        tau = jnp.zeros((ROWS, LANES), F32)
        top = jnp.ones((ROWS, LANES), F32)
        for k in range(depth):
            if m:
                wait_recv(second(k))
            p, l = k // share, k % share
            u = f_recv[m, p, l]
            v = f_recv[m, p, share + l]
            v_s = jnp.where(row == 0, f_recv[m, p, 2 * share, l : l + 1, :], pltpu.roll(v, 1, 0))
            u_w = jnp.where(lane == 0, f_recv[m, p, 2 * share + 1, :, l : l + 1], pltpu.roll(u, 1, 1))
            a_e = -0.5 * jnp.minimum(u, 0.0)
            a_w = 0.5 * jnp.maximum(u_w, 0.0)
            a_n = -0.5 * jnp.minimum(v, 0.0)
            a_s = 0.5 * jnp.maximum(v_s, 0.0)
            a_0 = 1.0 - 0.5 * (
                (jnp.maximum(u, 0.0) - jnp.minimum(u_w, 0.0)) + (jnp.maximum(v, 0.0) - jnp.minimum(v_s, 0.0))
            )
            sides = jnp.where(lane % 2 == 0, pltpu.roll(got_w[m, k], 1, 1), pltpu.roll(got_e[m, k], LANES - 1, 1))
            parts = []
            for t in range(tracers):
                x = source[t, k]
                edge = pltpu.roll(sides, (LANES - 2 * t) % LANES, 1)
                x_n = jnp.where(row == ROWS - 1, got_n[m, k, t : t + 1, :], pltpu.roll(x, ROWS - 1, 0))
                x_s = jnp.where(row == 0, got_s[m, k, t : t + 1, :], pltpu.roll(x, 1, 0))
                x_e = jnp.where(lane == LANES - 1, edge, pltpu.roll(x, LANES - 1, 1))
                x_w = jnp.where(lane == 0, edge, pltpu.roll(x, 1, 1))
                parts.append(a_0 * x + (a_e * x_e + a_w * x_w) + (a_n * x_n + a_s * x_s))
            adv = jnp.concatenate(parts, axis=0)
            wet_k = (k < depth_here).astype(F32)
            tau = tau + (0.1 + 0.3 * jnp.maximum(parts[0], 0.0))
            below = jnp.exp(-tau)
            h_send[m, p, l] = 2.0 * wet_k * (top - below)
            hi = adv.astype(jnp.bfloat16)
            lo = (adv - hi.astype(F32)).astype(jnp.bfloat16)
            both = jnp.dot(rates_hi, jnp.concatenate([hi, lo], axis=1), preferred_element_type=F32)
            r = both[:, :LANES] + both[:, LANES:] + jnp.dot(rates_lo, hi, preferred_element_type=F32)
            new = wet_k * (adv.reshape(tracers, ROWS, LANES) + (0.5 * top) * r.reshape(tracers, ROWS, LANES))
            target[:, k] = new
            if m == 0:
                pack(1, k, new)
                start(second(k))
            top = below
        for c in heats(m):
            c.start()
        h_recv[m, col] = h_send[m, col]

    wait_recv(first)
    for c in faces(0):
        c.wait_recv()
    tile_step(0, c_in, c_mid)
    for c in faces(1):
        c.wait_recv()
    tile_step(1, c_mid, c_out)

    for c in heats(0):
        c.wait_recv()
    for p in range(nlon):
        cols = slice(p * LANES, (p + 1) * LANES)
        t_out[:, :, cols] = t_base[:, :, cols] + 0.5 * wet_strip[:, :, cols] * h_recv[0, p]
    wait_send(dyn)
    wait_send(first)
    for k in range(depth):
        wait_send(second(k))
    for m in range(2):
        for c in faces(m):
            c.wait_send()
        for c in heats(m):
            c.wait_send()
    for c in heats(1):
        c.wait_recv()
    for p in range(nlon):
        h_out[:, :, p * LANES : (p + 1) * LANES] = h_recv[1, p]


def shards(sizes, u, v, t, h, c, n, r):
    tracers, depth, share, nlon, _, _ = sizes
    strip = jax.ShapeDtypeStruct(u.shape, F32)
    tile = (ROWS, LANES)
    strip_buf = pltpu.VMEM(u.shape, F32)
    dma = pltpu.SemaphoreType.DMA
    vmem = pl.BlockSpec(memory_space=pltpu.VMEM)
    return pl.pallas_call(
        functools.partial(kernel, sizes),
        out_shape=(strip, strip, strip, strip, jax.ShapeDtypeStruct(c.shape, F32)),
        in_specs=[vmem] * 7,
        out_specs=(vmem,) * 5,
        scratch_shapes=[
            strip_buf, strip_buf, strip_buf, strip_buf,
            pltpu.VMEM(n.shape, jnp.int32), pltpu.VMEM(n.shape, jnp.int32),
            pltpu.VMEM((4, share, EXT, u.shape[2]), F32),
            pltpu.VMEM((EXT, u.shape[2]), jnp.int32),
            strip_buf, strip_buf,
            pltpu.VMEM(c.shape, F32),
            pltpu.VMEM((2, depth, tracers, LANES), F32),
            pltpu.VMEM((2, depth, tracers, LANES), F32),
            pltpu.VMEM((2, depth) + tile, F32),
            pltpu.VMEM((2, depth, tracers, LANES), F32),
            pltpu.VMEM((2, depth, tracers, LANES), F32),
            pltpu.VMEM((2, depth) + tile, F32),
            pltpu.VMEM((2, depth) + tile, F32),
            pltpu.VMEM((2, nlon, 2 * share + 2) + tile, F32),
            pltpu.VMEM((2, nlon, 2 * share + 2) + tile, F32),
            pltpu.VMEM((2, nlon, share) + tile, F32),
            pltpu.VMEM((2, nlon, share) + tile, F32),
            dma((4,)), dma((4,)), dma((4,)), dma((4,)),
            dma((4, depth)), dma((4, depth)),
            dma((2, nlon)), dma((2, nlon)), dma((2, nlon)), dma((2, nlon)),
        ],
        compiler_params=pltpu.CompilerParams(
            collective_id=0, has_side_effects=True, vmem_limit_bytes=32 * 1024 * 1024
        ),
    )(u, v, t, h, c, n, r)


def solution(mesh):
    nlon, nrole = mesh.shape["lon"], mesh.shape["role"]
    nstrip = mesh.shape["lat"] * nrole
    strip = P("lon", ("grp", "lat", "role"), None)
    tile = P(None, None, ("grp", "lat", "role"), "lon")

    def run(u, v, t, h, c, n, r):
        sizes = (c.shape[0], c.shape[1], u.shape[0] // nlon, nlon, nrole, nstrip)
        return jax.shard_map(
            functools.partial(shards, sizes),
            mesh=mesh,
            in_specs=(strip, strip, strip, strip, tile, P(("grp", "lat", "role"), None), P()),
            out_specs=(strip, strip, strip, strip, tile),
            check_vma=False,
        )(u, v, t, h, c, n, r)

    return run
```

time: 120 us -> 27.7 us (0.23); the launches traced: 118 us -> 27.2 us
  starting transfers between devices: 40.7 us -> 0 us
  waiting for transfers between devices: 25.1 us -> 0 us
  local copies, waits for them, and re-layouts: 30.7 us -> 8.9 us
  Pallas kernels: 0 us -> 17.7 us
  other arithmetic: 17.3 us -> 0 us
  matrix products: 2.5 us -> 0 us
    ppermute x13 -> x0, starting transfers between devices: 27.1 us -> none  [the longest x6 17.9 us: padded(): before = lax.ppermute(last, axis, up)]
    pallas_call x0 -> x1, Pallas kernels: none -> 17.7 us  [shards(): pl.pallas_call(functools.partial(kernel, sizes), out_shape=(strip, strip,...]
    all_to_all x4 -> x0, starting transfers between devices: 13.6 us -> none  [the longest x2 6.85 us: shards(): lax.all_to_all(heat_tile, 'lon', split_axis=0, concat_axis=2, tiled=True)]
    all_to_all x4 -> x0, waiting for transfers between devices: 13.2 us -> none  [the longest x2 7.52 us: shards(): lax.all_to_all(jnp.stack([eastward_current, poleward_current]), 'lon', sp...]
    ppermute x13 -> x0, waiting for transfers between devices: 11.9 us -> none  [the longest x6 11.1 us: padded(): after = lax.ppermute(leading, axis, down)]
    slice x11 -> x0, local copies, waits for them, and re-layouts: 10.7 us -> none  [the longest x5 8.04 us: padded(): last = lax.slice_in_dim(shard, length - width, length, axis=dim)]
    ppermute x4 -> x0, local copies, waits for them, and re-layouts: 8.4 us -> none  [the longest x2 5.2 us: padded(): after = lax.ppermute(leading, axis, down)]
    mul x8 -> x0, other arithmetic: 5.06 us -> none  [the longest x4 3.33 us: tracer_step(): return (ocean_mask * (advected + 0.5 * top * react), thermal_energy)]
  transfers between devices with their start and end apart: 17 -> 0, of which waited for: 9 -> 0; matrix products, arithmetic and copies ran while one was open for 13% -> 0% of each run, Pallas kernels for 0% -> 0%
where the time goes in v1:
time: 27.7 us; the launch traced here: 27.2 us
  Pallas kernels  17.7 us (64%)
  local copies, waits for them, and re-layouts  8.9 us (32%)
  between operations  0.66 us (2%)
    pallas_call x1, Pallas kernels, shards(): pl.pallas_call(functools.partial(kernel, sizes), out_shape=(strip, strip,...  17.7 us
    unnamed x19, local copies, waits for them, and re-layouts  8.9 us

profile of v1, /device:TPU:0, one launch (start us, length us, event | category | flops | bytes accessed | tf_op | source)
XLA Modules:
  0.0 27.2 jit_solution(12128948656631148797)
XLA Ops:
  0.6 0.0 copy-start
  0.6 1.1 %copy-done = f32[24,8,8,128]{3,2,1,0:T(8,128)S(1)} copy-done((f32[24,8,8,128]{3,2,1,0:T(8,128)S(1)}, f32[24,8,8,128]{3,2,1,0:T(8,128)}, u32[]{:S(2)}) %copy-start) | copy-done | bytes 786456
  1.8 0.0 copy-start.1
  1.8 0.8 %copy-done.1 = f32[4,8,256]{2,1,0:T(8,128)S(1)} copy-done((f32[4,8,256]{2,1,0:T(8,128)S(1)}, f32[4,8,256]{2,1,0:T(8,128)}, u32[]{:S(2)}) %copy-start.1) | copy-done | bytes 32792
  2.5 0.0 copy-start.2
  2.5 0.8 %copy-done.2 = f32[4,8,256]{2,1,0:T(8,128)S(1)} copy-done((f32[4,8,256]{2,1,0:T(8,128)S(1)}, f32[4,8,256]{2,1,0:T(8,128)}, u32[]{:S(2)}) %copy-start.2) | copy-done | bytes 32792
  3.3 0.0 copy-start.3
  3.3 0.8 %copy-done.3 = f32[4,8,256]{2,1,0:T(8,128)S(1)} copy-done((f32[4,8,256]{2,1,0:T(8,128)S(1)}, f32[4,8,256]{2,1,0:T(8,128)}, u32[]{:S(2)}) %copy-start.3) | copy-done | bytes 32792
  4.0 0.0 copy-start.4
  4.0 0.8 %copy-done.4 = f32[4,8,256]{2,1,0:T(8,128)S(1)} copy-done((f32[4,8,256]{2,1,0:T(8,128)S(1)}, f32[4,8,256]{2,1,0:T(8,128)}, u32[]{:S(2)}) %copy-start.4) | copy-done | bytes 32792
  4.8 0.0 copy-start.5
  4.8 0.7 %copy-done.5 = f32[24,24]{1,0:T(8,128)S(1)} copy-done((f32[24,24]{1,0:T(8,128)S(1)}, f32[24,24]{1,0:T(8,128)}, u32[]{:S(2)}) %copy-start.5) | copy-done | bytes 2328
  5.5 0.0 copy-start.6
  5.5 0.7 %copy-done.6 = s32[8,256]{1,0:T(8,128)S(1)} copy-done((s32[8,256]{1,0:T(8,128)S(1)}, s32[8,256]{1,0:T(8,128)}, u32[]{:S(2)}) %copy-start.6) | copy-done | bytes 8216
  6.2 17.7 %shard_map.110 = (f32[4,8,256]{2,1,0:T(8,128)S(1)}, f32[4,8,256]{2,1,0:T(8,128)S(1)}, f32[4,8,256]{2,1,0:T(8,128)S(1)}, f32[4,8,256]{2,1,0:T(8,128)S(1)}, f32[24,8,8,128]{3,2,1,0:T(8,128)S(1)}) custom-call(f32[4,8,256]{2,1,0:T(8,128)S(1)} %copy-done.1, f32[4,8,256]{2,1,0:T(8,128)S(1)} %copy-done.2, f32[4,8,256]{2,1,0:T(8,128)S(1)} %copy-done.3, ...), custom_call_target="tpu_custom_call" | custom-call | tf_op jit(solution)/shard_map/pallas_call | solution.py:342
  23.9 0.6 %copy.17 = f32[4,8,256]{2,1,0:T(8,128)} copy(f32[4,8,256]{2,1,0:T(8,128)S(1)} %get-tuple-element.10) | data formatting | bytes 65536
  24.5 0.6 %copy.18 = f32[4,8,256]{2,1,0:T(8,128)} copy(f32[4,8,256]{2,1,0:T(8,128)S(1)} %get-tuple-element.11) | data formatting | bytes 65536
  25.1 0.6 %copy.19 = f32[4,8,256]{2,1,0:T(8,128)} copy(f32[4,8,256]{2,1,0:T(8,128)S(1)} %get-tuple-element.12) | data formatting | bytes 65536
  25.7 0.6 %copy.20 = f32[4,8,256]{2,1,0:T(8,128)} copy(f32[4,8,256]{2,1,0:T(8,128)S(1)} %get-tuple-element.13) | data formatting | bytes 65536
  26.3 0.9 %copy.21 = f32[24,8,8,128]{3,2,1,0:T(8,128)} copy(f32[24,8,8,128]{3,2,1,0:T(8,128)S(1)} %get-tuple-element.14) | data formatting | bytes 1572864
Async XLA Ops:
  0.6 1.1 %copy-start = (f32[24,8,8,128]{3,2,1,0:T(8,128)S(1)}, f32[24,8,8,128]{3,2,1,0:T(8,128)}, u32[]{:S(2)}) copy-start(f32[24,8,8,128]{3,2,1,0:T(8,128)} %c_in.1) | copy-start | bytes 2359300
  1.8 0.8 %copy-start.1 = (f32[4,8,256]{2,1,0:T(8,128)S(1)}, f32[4,8,256]{2,1,0:T(8,128)}, u32[]{:S(2)}) copy-start(f32[4,8,256]{2,1,0:T(8,128)} %u_in.1) | copy-start | bytes 98308
  2.5 0.8 %copy-start.2 = (f32[4,8,256]{2,1,0:T(8,128)S(1)}, f32[4,8,256]{2,1,0:T(8,128)}, u32[]{:S(2)}) copy-start(f32[4,8,256]{2,1,0:T(8,128)} %v_in.1) | copy-start | bytes 98308
  3.3 0.8 %copy-start.3 = (f32[4,8,256]{2,1,0:T(8,128)S(1)}, f32[4,8,256]{2,1,0:T(8,128)}, u32[]{:S(2)}) copy-start(f32[4,8,256]{2,1,0:T(8,128)} %t_in.1) | copy-start | bytes 98308
  4.0 0.8 %copy-start.4 = (f32[4,8,256]{2,1,0:T(8,128)S(1)}, f32[4,8,256]{2,1,0:T(8,128)}, u32[]{:S(2)}) copy-start(f32[4,8,256]{2,1,0:T(8,128)} %h_in.1) | copy-start | bytes 98308
  4.8 0.7 %copy-start.5 = (f32[24,24]{1,0:T(8,128)S(1)}, f32[24,24]{1,0:T(8,128)}, u32[]{:S(2)}) copy-start(f32[24,24]{1,0:T(8,128)} %r_in.1) | copy-start | bytes 6916
  5.5 0.7 %copy-start.6 = (s32[8,256]{1,0:T(8,128)S(1)}, s32[8,256]{1,0:T(8,128)}, u32[]{:S(2)}) copy-start(s32[8,256]{1,0:T(8,128)} %n_in.1) | copy-start | bytes 24580

commit v2 on v1

--- a/solution.py
+++ b/solution.py
@@ -11,6 +11,9 @@
 LANES = 128
 PAD = 4
 EXT = ROWS + 2 * PAD
+EARLY = 5
+VMEM = 64 * 1024 * 1024
+CUTS = 4
 F32 = jnp.float32
 
 
@@ -38,15 +41,23 @@
 
 def kernel(
     sizes,
-    u_in, v_in, t_in, h_in, c_in, n_in, r_in,
-    u_out, v_out, t_out, h_out, c_out,
+    u_hbm, v_hbm, t_hbm, h_hbm, c_hbm, n_hbm, r_hbm,
+    u_dst, v_dst, t_dst, h_dst, c_dst,
     pk_n, pk_s, rc_n, rc_s, cnt_n, cnt_s, ext, ext_n, t_base, wet_strip,
     c_mid, row_lo, row_hi, col_ed, got_n, got_s, got_w, got_e,
     f_send, f_recv, h_send, h_recv,
+    u_in, v_in, t_in, h_in, c_in, n_in, r_in, in_sem,
+    u_out, v_out, t_out, h_out, c_out, out_sem,
     d_ssem, d_rsem, c0_ssem, c0_rsem, c1_ssem, c1_rsem, f_ssem, f_rsem, h_ssem, h_rsem,
 ):
     tracers, depth, share, nlon, nrole, nstrip = sizes
     width = nlon * LANES
+    arrays = (
+        (u_hbm, u_in), (v_hbm, v_in), (t_hbm, t_in), (h_hbm, h_in), (n_hbm, n_in), (c_hbm, c_in), (r_hbm, r_in),
+    )
+    loads = [pltpu.make_async_copy(a, b, in_sem.at[i]) for i, (a, b) in enumerate(arrays)]
+    for load in loads:
+        load.start()
     s = lax.axis_index("lat") * nrole + lax.axis_index("role")
     col = lax.axis_index("lon")
     has_n, has_s = s < nstrip - 1, s > 0
@@ -85,6 +96,8 @@
         for c, send, _ in copies:
             pl.when(send)(c.wait_send)
 
+    for load in loads[:5]:
+        load.wait()
     pk_n[:, 0:3, :] = v_in[:, 5:8, :]
     pk_n[:, 3:5, :] = u_in[:, 6:8, :]
     pk_n[:, 5:7, :] = t_in[:, 6:8, :]
@@ -106,9 +119,6 @@
             here = (lane == 2 * t - 1) | (lane == 2 * t)
             acc = jnp.where(here, pltpu.roll(x[t], 2 * t, 1), acc)
         col_ed[m, k] = acc
-
-    for k in range(depth):
-        pack(0, k, c_in[:, k])
 
     dyn = [
         (copy(pk_n, rc_s, d_ssem.at[0], d_rsem.at[0], dev_n), has_n, has_s),
@@ -147,6 +157,10 @@
 
     pl.semaphore_wait(barrier, nlon - 1 + jnp.minimum(s, 1) + jnp.minimum(nstrip - 1 - s, 1))
     start(dyn)
+    for load in loads[5:]:
+        load.wait()
+    for k in range(depth):
+        pack(0, k, c_in[:, k])
     start(first)
 
     @pl.when(jnp.logical_not(has_s))
@@ -250,17 +264,25 @@
     t1 = wet * (t0 + 0.1 * lap(t0) + 0.5 * ext[3])
     u2, v2 = advance(u1, v1, t1)
     publish(1, u2, v2)
+    saves = [
+        pltpu.make_async_copy(a, b, out_sem.at[i])
+        for i, (a, b) in enumerate(((u_out, u_dst), (v_out, v_dst), (t_out, t_dst), (h_out, h_dst)))
+    ]
+    saves += [pltpu.make_async_copy(c_out.at[:, k], c_dst.at[:, k], out_sem.at[4 + k]) for k in range(depth)]
     u_out[...] = u2[:, PAD : PAD + ROWS, :]
     v_out[...] = v2[:, PAD : PAD + ROWS, :]
+    saves[0].start()
+    saves[1].start()
     t_base[...] = (wet * (t1 + 0.1 * lap(t1)))[:, PAD : PAD + ROWS, :]
     wet_strip[...] = wet[:, PAD : PAD + ROWS, :]
 
     depth_here = n_in[:, pl.ds(pl.multiple_of(col * LANES, LANES), LANES)]
 
     def tile_step(m, source, target):
-        tau = jnp.zeros((ROWS, LANES), F32)
-        top = jnp.ones((ROWS, LANES), F32)
-        for k in range(depth):
+        coefs, sides, light = {}, {}, {}
+        state = [jnp.zeros((ROWS, LANES), F32), jnp.ones((ROWS, LANES), F32)]
+
+        def prepare(k):
             if m:
                 wait_recv(second(k))
             p, l = k // share, k % share
@@ -268,28 +290,49 @@
             v = f_recv[m, p, share + l]
             v_s = jnp.where(row == 0, f_recv[m, p, 2 * share, l : l + 1, :], pltpu.roll(v, 1, 0))
             u_w = jnp.where(lane == 0, f_recv[m, p, 2 * share + 1, :, l : l + 1], pltpu.roll(u, 1, 1))
-            a_e = -0.5 * jnp.minimum(u, 0.0)
-            a_w = 0.5 * jnp.maximum(u_w, 0.0)
-            a_n = -0.5 * jnp.minimum(v, 0.0)
-            a_s = 0.5 * jnp.maximum(v_s, 0.0)
             a_0 = 1.0 - 0.5 * (
                 (jnp.maximum(u, 0.0) - jnp.minimum(u_w, 0.0)) + (jnp.maximum(v, 0.0) - jnp.minimum(v_s, 0.0))
             )
-            sides = jnp.where(lane % 2 == 0, pltpu.roll(got_w[m, k], 1, 1), pltpu.roll(got_e[m, k], LANES - 1, 1))
-            parts = []
-            for t in range(tracers):
-                x = source[t, k]
-                edge = pltpu.roll(sides, (LANES - 2 * t) % LANES, 1)
-                x_n = jnp.where(row == ROWS - 1, got_n[m, k, t : t + 1, :], pltpu.roll(x, ROWS - 1, 0))
-                x_s = jnp.where(row == 0, got_s[m, k, t : t + 1, :], pltpu.roll(x, 1, 0))
-                x_e = jnp.where(lane == LANES - 1, edge, pltpu.roll(x, LANES - 1, 1))
-                x_w = jnp.where(lane == 0, edge, pltpu.roll(x, 1, 1))
-                parts.append(a_0 * x + (a_e * x_e + a_w * x_w) + (a_n * x_n + a_s * x_s))
-            adv = jnp.concatenate(parts, axis=0)
+            coefs[k] = (
+                a_0, -0.5 * jnp.minimum(u, 0.0), 0.5 * jnp.maximum(u_w, 0.0),
+                -0.5 * jnp.minimum(v, 0.0), 0.5 * jnp.maximum(v_s, 0.0),
+            )
+            sides[k] = jnp.where(
+                lane % 2 == 0, pltpu.roll(got_w[m, k], 1, 1), pltpu.roll(got_e[m, k], LANES - 1, 1)
+            )
+
+        def advect(k, t):
+            a_0, a_e, a_w, a_n, a_s = coefs[k]
+            x = source[t, k]
+            edge = pltpu.roll(sides[k], (LANES - 2 * t) % LANES, 1)
+            x_n = jnp.where(row == ROWS - 1, got_n[m, k, t : t + 1, :], pltpu.roll(x, ROWS - 1, 0))
+            x_s = jnp.where(row == 0, got_s[m, k, t : t + 1, :], pltpu.roll(x, 1, 0))
+            x_e = jnp.where(lane == LANES - 1, edge, pltpu.roll(x, LANES - 1, 1))
+            x_w = jnp.where(lane == 0, edge, pltpu.roll(x, 1, 1))
+            return a_0 * x + (a_e * x_e + a_w * x_w) + (a_n * x_n + a_s * x_s)
+
+        def shine(k):
+            p, l = k // share, k % share
+            prepare(k)
+            lead = advect(k, 0)
             wet_k = (k < depth_here).astype(F32)
-            tau = tau + (0.1 + 0.3 * jnp.maximum(parts[0], 0.0))
+            tau, top = state
+            tau = tau + (0.1 + 0.3 * jnp.maximum(lead, 0.0))
             below = jnp.exp(-tau)
             h_send[m, p, l] = 2.0 * wet_k * (top - below)
+            light[k] = (lead, wet_k, top)
+            state[:] = [tau, below]
+            if k == depth - 1:
+                for c in heats(m):
+                    c.start()
+                h_recv[m, col] = h_send[m, col]
+
+        for k in range(depth):
+            if k not in light:
+                for ahead in range(k, depth if m and k >= EARLY else k + 1):
+                    shine(ahead)
+            lead, wet_k, top = light[k]
+            adv = jnp.concatenate([lead] + [advect(k, t) for t in range(1, tracers)], axis=0)
             hi = adv.astype(jnp.bfloat16)
             lo = (adv - hi.astype(F32)).astype(jnp.bfloat16)
             both = jnp.dot(rates_hi, jnp.concatenate([hi, lo], axis=1), preferred_element_type=F32)
@@ -299,10 +342,8 @@
             if m == 0:
                 pack(1, k, new)
                 start(second(k))
-            top = below
-        for c in heats(m):
-            c.start()
-        h_recv[m, col] = h_send[m, col]
+            else:
+                saves[4 + k].start()
 
     wait_recv(first)
     for c in faces(0):
@@ -317,6 +358,7 @@
     for p in range(nlon):
         cols = slice(p * LANES, (p + 1) * LANES)
         t_out[:, :, cols] = t_base[:, :, cols] + 0.5 * wet_strip[:, :, cols] * h_recv[0, p]
+    saves[2].start()
     wait_send(dyn)
     wait_send(first)
     for k in range(depth):
@@ -330,6 +372,24 @@
         c.wait_recv()
     for p in range(nlon):
         h_out[:, :, p * LANES : (p + 1) * LANES] = h_recv[1, p]
+    saves[3].start()
+    for save in saves:
+        save.wait()
+
+
+def store(*refs):
+    half = len(refs) // 2
+    sems = refs[-1]
+    cut = refs[half - 1].shape[0] // CUTS
+    pairs = list(zip(refs[: half - 1], refs[half : 2 * half - 1]))
+    for i in range(CUTS):
+        piece = slice(i * cut, (i + 1) * cut)
+        pairs.append((refs[half - 1].at[piece], refs[2 * half - 1].at[piece]))
+    copies = [pltpu.make_async_copy(a, b, sems.at[i]) for i, (a, b) in enumerate(pairs)]
+    for c in copies:
+        c.start()
+    for c in copies:
+        c.wait()
 
 
 def shards(sizes, u, v, t, h, c, n, r):
@@ -338,12 +398,12 @@
     tile = (ROWS, LANES)
     strip_buf = pltpu.VMEM(u.shape, F32)
     dma = pltpu.SemaphoreType.DMA
-    vmem = pl.BlockSpec(memory_space=pltpu.VMEM)
-    return pl.pallas_call(
+    hbm = pl.BlockSpec(memory_space=pltpu.HBM)
+    outs = pl.pallas_call(
         functools.partial(kernel, sizes),
         out_shape=(strip, strip, strip, strip, jax.ShapeDtypeStruct(c.shape, F32)),
-        in_specs=[vmem] * 7,
-        out_specs=(vmem,) * 5,
+        in_specs=[hbm] * 7,
+        out_specs=(hbm,) * 5,
         scratch_shapes=[
             strip_buf, strip_buf, strip_buf, strip_buf,
             pltpu.VMEM(n.shape, jnp.int32), pltpu.VMEM(n.shape, jnp.int32),
@@ -362,14 +422,25 @@
             pltpu.VMEM((2, nlon, 2 * share + 2) + tile, F32),
             pltpu.VMEM((2, nlon, share) + tile, F32),
             pltpu.VMEM((2, nlon, share) + tile, F32),
+            strip_buf, strip_buf, strip_buf, strip_buf, pltpu.VMEM(c.shape, F32),
+            pltpu.VMEM(n.shape, jnp.int32), pltpu.VMEM(r.shape, F32), dma((7,)),
+            strip_buf, strip_buf, strip_buf, strip_buf, pltpu.VMEM(c.shape, F32), dma((4 + c.shape[1],)),
             dma((4,)), dma((4,)), dma((4,)), dma((4,)),
             dma((4, depth)), dma((4, depth)),
             dma((2, nlon)), dma((2, nlon)), dma((2, nlon)), dma((2, nlon)),
         ],
         compiler_params=pltpu.CompilerParams(
-            collective_id=0, has_side_effects=True, vmem_limit_bytes=32 * 1024 * 1024
+            collective_id=0, has_side_effects=True, vmem_limit_bytes=VMEM
         ),
     )(u, v, t, h, c, n, r)
+    return pl.pallas_call(
+        store,
+        out_shape=(strip, strip, strip, strip, jax.ShapeDtypeStruct(c.shape, F32)),
+        in_specs=[pl.BlockSpec(memory_space=pl.ANY)] * 5,
+        out_specs=(hbm,) * 5,
+        scratch_shapes=[dma((4 + CUTS,))],
+        compiler_params=pltpu.CompilerParams(vmem_limit_bytes=VMEM),
+    )(*outs)
 
 
 def solution(mesh):

time: 27.7 us -> 48.1 us (1.74)
  Pallas kernels: 17.7 us -> 47.3 us
  local copies, waits for them, and re-layouts: 8.9 us -> 0 us
    pallas_call x0 -> x1, Pallas kernels: none -> 29 us  [shards(): pl.pallas_call(store, out_shape=(strip, strip, strip, strip, jax.ShapeDty...]
    unnamed x19 -> x0, local copies, waits for them, and re-layouts: 8.9 us -> none
    pallas_call x1, Pallas kernels: 17.7 us -> 18.3 us  [shards(): pl.pallas_call(functools.partial(kernel, sizes), out_shape=(strip, strip,...]
where the time goes in v2:
time: 48.1 us; the launch traced here: 48 us
  Pallas kernels  47.3 us (98%)
  between operations  0.64 us (1%)
    pallas_call x1, Pallas kernels, shards(): pl.pallas_call(store, out_shape=(strip, strip, strip, strip, jax.ShapeDty...  29 us
    pallas_call x1, Pallas kernels, shards(): pl.pallas_call(functools.partial(kernel, sizes), out_shape=(strip, strip,...  18.3 us

profile of v2, /device:TPU:0, one launch (start us, length us, event | category | flops | bytes accessed | tf_op | source)
XLA Modules:
  0.0 48.0 jit_solution(2525942457392224634)
XLA Ops:
  0.6 18.3 %shard_map.110 = (f32[4,8,256]{2,1,0:T(8,128)}, f32[4,8,256]{2,1,0:T(8,128)}, f32[4,8,256]{2,1,0:T(8,128)}, f32[4,8,256]{2,1,0:T(8,128)}, f32[24,8,8,128]{3,2,1,0:T(8,128)}) custom-call(f32[4,8,256]{2,1,0:T(8,128)} %u_hbm.1, f32[4,8,256]{2,1,0:T(8,128)} %v_hbm.1, f32[4,8,256]{2,1,0:T(8,128)} %t_hbm.1, f32[4,8,256]{2,1,0:T(8,128)} %h_hbm.1, ...), custom_call_target="tpu_custom_call" | custom-call | tf_op jit(solution)/shard_map/pallas_call | solution.py:402
  19.0 29.0 %shard_map.111 = (f32[4,8,256]{2,1,0:T(8,128)}, f32[4,8,256]{2,1,0:T(8,128)}, f32[4,8,256]{2,1,0:T(8,128)}, f32[4,8,256]{2,1,0:T(8,128)}, f32[24,8,8,128]{3,2,1,0:T(8,128)}) custom-call(f32[4,8,256]{2,1,0:T(8,128)} %get-tuple-element.10.refs_0_, f32[4,8,256]{2,1,0:T(8,128)} %get-tuple-element.11.refs_1_, f32[4,8,256]{2,1,0:T(8,128)} %get-tuple-element.12.refs_2_, ...), custom_call_target="tpu_custom_call" | custom-call | tf_op jit(solution)/shard_map/pallas_call | solution.py:436

commit v3 on v2

--- a/solution.py
+++ b/solution.py
@@ -378,18 +378,22 @@
 
 
 def store(*refs):
-    half = len(refs) // 2
-    sems = refs[-1]
-    cut = refs[half - 1].shape[0] // CUTS
-    pairs = list(zip(refs[: half - 1], refs[half : 2 * half - 1]))
-    for i in range(CUTS):
-        piece = slice(i * cut, (i + 1) * cut)
-        pairs.append((refs[half - 1].at[piece], refs[2 * half - 1].at[piece]))
-    copies = [pltpu.make_async_copy(a, b, sems.at[i]) for i, (a, b) in enumerate(pairs)]
-    for c in copies:
-        c.start()
-    for c in copies:
-        c.wait()
+    half = len(refs) // 3
+    sources, results, held, (load_sem, save_sem) = refs[:half], refs[half : 2 * half], refs[2 * half : -2], refs[-2:]
+    cut = sources[-1].shape[0] // CUTS
+    pieces = [(i, slice(None)) for i in range(half - 1)]
+    pieces = [(half - 1, slice(i * cut, (i + 1) * cut)) for i in range(CUTS)] + pieces
+    loads, saves = [], []
+    for n, (i, piece) in enumerate(pieces):
+        loads.append(pltpu.make_async_copy(sources[i].at[piece], held[i].at[piece], load_sem.at[n]))
+        saves.append(pltpu.make_async_copy(held[i].at[piece], results[i].at[piece], save_sem.at[n]))
+    for load in loads:
+        load.start()
+    for load, save in zip(loads, saves):
+        load.wait()
+        save.start()
+    for save in saves:
+        save.wait()
 
 
 def shards(sizes, u, v, t, h, c, n, r):
@@ -436,9 +440,9 @@
     return pl.pallas_call(
         store,
         out_shape=(strip, strip, strip, strip, jax.ShapeDtypeStruct(c.shape, F32)),
-        in_specs=[pl.BlockSpec(memory_space=pl.ANY)] * 5,
+        in_specs=[hbm] * 5,
         out_specs=(hbm,) * 5,
-        scratch_shapes=[dma((4 + CUTS,))],
+        scratch_shapes=[strip_buf] * 4 + [pltpu.VMEM(c.shape, F32), dma((4 + CUTS,)), dma((4 + CUTS,))],
         compiler_params=pltpu.CompilerParams(vmem_limit_bytes=VMEM),
     )(*outs)
 

time: 48.1 us -> 21.2 us (0.44)
  Pallas kernels: 47.3 us -> 20.4 us
    pallas_call x1, Pallas kernels: 29 us -> 2.07 us  [shards(): pl.pallas_call(store, out_shape=(strip, strip, strip, strip, jax.ShapeDty...]
where the time goes in v3:
time: 21.2 us; the launch traced here: 21.1 us
  Pallas kernels  20.4 us (96%)
  between operations  0.64 us (3%)
    pallas_call x1, Pallas kernels, shards(): pl.pallas_call(functools.partial(kernel, sizes), out_shape=(strip, strip,...  18.3 us
    pallas_call x1, Pallas kernels, shards(): pl.pallas_call(store, out_shape=(strip, strip, strip, strip, jax.ShapeDty...  2.07 us

profile of v3, /device:TPU:0, one launch (start us, length us, event | category | flops | bytes accessed | tf_op | source)
XLA Modules:
  0.0 21.1 jit_solution(11490187588623845527)
XLA Ops:
  0.6 18.3 %shard_map.110 = (f32[4,8,256]{2,1,0:T(8,128)}, f32[4,8,256]{2,1,0:T(8,128)}, f32[4,8,256]{2,1,0:T(8,128)}, f32[4,8,256]{2,1,0:T(8,128)}, f32[24,8,8,128]{3,2,1,0:T(8,128)}) custom-call(f32[4,8,256]{2,1,0:T(8,128)} %u_hbm.1, f32[4,8,256]{2,1,0:T(8,128)} %v_hbm.1, f32[4,8,256]{2,1,0:T(8,128)} %t_hbm.1, f32[4,8,256]{2,1,0:T(8,128)} %h_hbm.1, ...), custom_call_target="tpu_custom_call" | custom-call | tf_op jit(solution)/shard_map/pallas_call | solution.py:406
  19.0 2.1 %shard_map.111 = (f32[4,8,256]{2,1,0:T(8,128)}, f32[4,8,256]{2,1,0:T(8,128)}, f32[4,8,256]{2,1,0:T(8,128)}, f32[4,8,256]{2,1,0:T(8,128)}, f32[24,8,8,128]{3,2,1,0:T(8,128)}) custom-call(f32[4,8,256]{2,1,0:T(8,128)} %get-tuple-element.10.refs_0_, f32[4,8,256]{2,1,0:T(8,128)} %get-tuple-element.11.refs_1_, f32[4,8,256]{2,1,0:T(8,128)} %get-tuple-element.12.refs_2_, ...), custom_call_target="tpu_custom_call" | custom-call | tf_op jit(solution)/shard_map/pallas_call | solution.py:440

commit v4 on v3

--- a/solution.py
+++ b/solution.py
@@ -11,9 +11,9 @@
 LANES = 128
 PAD = 4
 EXT = ROWS + 2 * PAD
-EARLY = 5
+PAIR = 2
 VMEM = 64 * 1024 * 1024
-CUTS = 4
+CUTS = 8
 F32 = jnp.float32
 
 
@@ -133,12 +133,15 @@
         (copy(col_ed.at[0], got_e.at[0], c0_ssem.at[3], c0_rsem.at[3], dev_w), has_w, has_e),
     ]
 
-    def second(k):
+    def second(g):
+        two = pl.ds(g * PAIR, PAIR)
+        routes = (
+            (row_hi, got_s, dev_n, has_n, has_s), (row_lo, got_n, dev_s, has_s, has_n),
+            (col_ed, got_w, dev_e, has_e, has_w), (col_ed, got_e, dev_w, has_w, has_e),
+        )
         return [
-            (copy(row_hi.at[1, k], got_s.at[1, k], c1_ssem.at[0, k], c1_rsem.at[0, k], dev_n), has_n, has_s),
-            (copy(row_lo.at[1, k], got_n.at[1, k], c1_ssem.at[1, k], c1_rsem.at[1, k], dev_s), has_s, has_n),
-            (copy(col_ed.at[1, k], got_w.at[1, k], c1_ssem.at[2, k], c1_rsem.at[2, k], dev_e), has_e, has_w),
-            (copy(col_ed.at[1, k], got_e.at[1, k], c1_ssem.at[3, k], c1_rsem.at[3, k], dev_w), has_w, has_e),
+            (copy(a.at[1, two], b.at[1, two], c1_ssem.at[i, g], c1_rsem.at[i, g], dev), send, recv)
+            for i, (a, b, dev, send, recv) in enumerate(routes)
         ]
 
     def faces(m):
@@ -283,8 +286,6 @@
         state = [jnp.zeros((ROWS, LANES), F32), jnp.ones((ROWS, LANES), F32)]
 
         def prepare(k):
-            if m:
-                wait_recv(second(k))
             p, l = k // share, k % share
             u = f_recv[m, p, l]
             v = f_recv[m, p, share + l]
@@ -327,23 +328,41 @@
                     c.start()
                 h_recv[m, col] = h_send[m, col]
 
-        for k in range(depth):
-            if k not in light:
-                for ahead in range(k, depth if m and k >= EARLY else k + 1):
-                    shine(ahead)
-            lead, wet_k, top = light[k]
-            adv = jnp.concatenate([lead] + [advect(k, t) for t in range(1, tracers)], axis=0)
-            hi = adv.astype(jnp.bfloat16)
-            lo = (adv - hi.astype(F32)).astype(jnp.bfloat16)
-            both = jnp.dot(rates_hi, jnp.concatenate([hi, lo], axis=1), preferred_element_type=F32)
-            r = both[:, :LANES] + both[:, LANES:] + jnp.dot(rates_lo, hi, preferred_element_type=F32)
-            new = wet_k * (adv.reshape(tracers, ROWS, LANES) + (0.5 * top) * r.reshape(tracers, ROWS, LANES))
-            target[:, k] = new
-            if m == 0:
-                pack(1, k, new)
-                start(second(k))
-            else:
-                saves[4 + k].start()
+        groups = depth // PAIR
+        held = {}
+        for g in range(groups + 1):
+            if g < groups:
+                if m:
+                    wait_recv(second(g))
+                levels = range(g * PAIR, (g + 1) * PAIR)
+                for k in levels:
+                    shine(k)
+                adv = [
+                    jnp.concatenate([light[k][0]] + [advect(k, t) for t in range(1, tracers)], axis=0)
+                    for k in levels
+                ]
+                hi = [a.astype(jnp.bfloat16) for a in adv]
+                lo = [(a - b.astype(F32)).astype(jnp.bfloat16) for a, b in zip(adv, hi)]
+                held[g] = (adv, jnp.concatenate(hi, axis=1), jnp.concatenate(lo, axis=1))
+            if g > 0:
+                adv, hi, lo = held.pop(g - 1)
+                r = (
+                    jnp.dot(rates_hi, hi, preferred_element_type=F32)
+                    + jnp.dot(rates_hi, lo, preferred_element_type=F32)
+                    + jnp.dot(rates_lo, hi, preferred_element_type=F32)
+                )
+                for n in range(PAIR):
+                    k = (g - 1) * PAIR + n
+                    _, wet_k, top = light[k]
+                    gain = r[:, n * LANES : (n + 1) * LANES].reshape(tracers, ROWS, LANES)
+                    new = wet_k * (adv[n].reshape(tracers, ROWS, LANES) + (0.5 * top) * gain)
+                    target[:, k] = new
+                    if m == 0:
+                        pack(1, k, new)
+                    else:
+                        saves[4 + k].start()
+                if m == 0:
+                    start(second(g - 1))
 
     wait_recv(first)
     for c in faces(0):
@@ -361,8 +380,8 @@
     saves[2].start()
     wait_send(dyn)
     wait_send(first)
-    for k in range(depth):
-        wait_send(second(k))
+    for g in range(depth // PAIR):
+        wait_send(second(g))
     for m in range(2):
         for c in faces(m):
             c.wait_send()

time: 21.2 us -> 19.4 us (0.915)
  Pallas kernels: 20.4 us -> 18.6 us
    pallas_call x1, Pallas kernels: 18.3 us -> 16.5 us  [shards(): pl.pallas_call(functools.partial(kernel, sizes), out_shape=(strip, strip,...]
where the time goes in v4:
time: 19.4 us; the launch traced here: 19.2 us
  Pallas kernels  18.6 us (96%)
  between operations  0.64 us (3%)
    pallas_call x1, Pallas kernels, shards(): pl.pallas_call(functools.partial(kernel, sizes), out_shape=(strip, strip,...  16.5 us
    pallas_call x1, Pallas kernels, shards(): pl.pallas_call(store, out_shape=(strip, strip, strip, strip, jax.ShapeDty...  2.11 us

profile of v4, /device:TPU:0, one launch (start us, length us, event | category | flops | bytes accessed | tf_op | source)
XLA Modules:
  0.0 19.2 jit_solution(18386982270361758212)
XLA Ops:
  0.6 16.5 %shard_map.110 = (f32[4,8,256]{2,1,0:T(8,128)}, f32[4,8,256]{2,1,0:T(8,128)}, f32[4,8,256]{2,1,0:T(8,128)}, f32[4,8,256]{2,1,0:T(8,128)}, f32[24,8,8,128]{3,2,1,0:T(8,128)}) custom-call(f32[4,8,256]{2,1,0:T(8,128)} %u_hbm.1, f32[4,8,256]{2,1,0:T(8,128)} %v_hbm.1, f32[4,8,256]{2,1,0:T(8,128)} %t_hbm.1, f32[4,8,256]{2,1,0:T(8,128)} %h_hbm.1, ...), custom_call_target="tpu_custom_call" | custom-call | tf_op jit(solution)/shard_map/pallas_call | solution.py:425
  17.1 2.1 %shard_map.111 = (f32[4,8,256]{2,1,0:T(8,128)}, f32[4,8,256]{2,1,0:T(8,128)}, f32[4,8,256]{2,1,0:T(8,128)}, f32[4,8,256]{2,1,0:T(8,128)}, f32[24,8,8,128]{3,2,1,0:T(8,128)}) custom-call(f32[4,8,256]{2,1,0:T(8,128)} %get-tuple-element.10.refs_0_, f32[4,8,256]{2,1,0:T(8,128)} %get-tuple-element.11.refs_1_, f32[4,8,256]{2,1,0:T(8,128)} %get-tuple-element.12.refs_2_, ...), custom_call_target="tpu_custom_call" | custom-call | tf_op jit(solution)/shard_map/pallas_call | solution.py:459

commit v5 on v4

--- a/solution.py
+++ b/solution.py
@@ -186,6 +186,77 @@
     def _():
         got_e[...] = jnp.zeros_like(got_e)
 
+    zero = jnp.zeros((share, PAD, width), F32)
+    for f in range(4):
+        ext[f, :, 0:PAD, :] = zero
+        ext[f, :, PAD + ROWS :, :] = zero
+    ext_n[0:PAD, :] = jnp.zeros((PAD, width), jnp.int32)
+    ext_n[PAD + ROWS :, :] = jnp.zeros((PAD, width), jnp.int32)
+    for f, ref in enumerate((u_in, v_in, t_in, h_in)):
+        ext[f, :, PAD : PAD + ROWS, :] = ref[...]
+    ext_n[PAD : PAD + ROWS, :] = n_in[...]
+
+    wait_recv(dyn)
+    ext[0, :, 2:4, :] = rc_s[:, 3:5, :]
+    ext[1, :, 1:4, :] = rc_s[:, 0:3, :]
+    ext[2, :, 2:4, :] = rc_s[:, 5:7, :]
+    ext[3, :, 3:4, :] = rc_s[:, 7:8, :]
+    ext[0, :, 12:14, :] = rc_n[:, 0:2, :]
+    ext[1, :, 12:14, :] = rc_n[:, 2:4, :]
+    ext[2, :, 12:14, :] = rc_n[:, 4:6, :]
+    ext[3, :, 12:13, :] = rc_n[:, 6:7, :]
+    ext_n[2:4, :] = cnt_s[6:8, :]
+    ext_n[12:14, :] = cnt_n[0:2, :]
+
+    shape = (share, EXT, width)
+    level = col * share + lax.broadcasted_iota(jnp.int32, shape, 0)
+    wet = (level < ext_n[...][None]).astype(F32)
+    wet_u = wet * east(wet)
+    wet_v = wet * north(wet)
+    spot = (s * ROWS - PAD + lax.broadcasted_iota(jnp.int32, shape, 1)).astype(F32)
+    fcor = 0.3 * (2.0 * (spot + 0.5) / (nstrip * ROWS) - 1.0)
+
+    def advance(u, v, t):
+        new_u = wet_u * (u + 0.1 * lap(u) + fcor * v - 0.2 * (east(t) - t))
+        new_v = wet_v * (v + 0.1 * lap(v) - fcor * u - 0.2 * (north(t) - t))
+        return new_u, new_v
+
+    def publish(m, u, v):
+        for p in range(nlon):
+            lo = p * LANES
+            cols = slice(lo, lo + LANES)
+            v_edge = jnp.zeros((ROWS, LANES), F32)
+            u_edge = jnp.zeros((ROWS, LANES), F32)
+            for l in range(share):
+                f_send[m, p, l] = u[l, PAD : PAD + ROWS, cols]
+                f_send[m, p, share + l] = v[l, PAD : PAD + ROWS, cols]
+                v_edge = jnp.where(row == l, v[l, PAD - 1 : PAD, cols], v_edge)
+                if p:
+                    u_edge = jnp.where(lane == l, u[l, PAD : PAD + ROWS, lo - 1 : lo], u_edge)
+            f_send[m, p, 2 * share] = v_edge
+            f_send[m, p, 2 * share + 1] = u_edge
+        for c in faces(m):
+            c.start()
+        f_recv[m, col] = f_send[m, col]
+
+    u0, v0, t0 = ext[0], ext[1], ext[2]
+    u1, v1 = advance(u0, v0, t0)
+    publish(0, u1, v1)
+    t1 = wet * (t0 + 0.1 * lap(t0) + 0.5 * ext[3])
+    u2, v2 = advance(u1, v1, t1)
+    publish(1, u2, v2)
+    saves = [
+        pltpu.make_async_copy(a, b, out_sem.at[i])
+        for i, (a, b) in enumerate(((u_out, u_dst), (v_out, v_dst), (t_out, t_dst), (h_out, h_dst)))
+    ]
+    saves += [pltpu.make_async_copy(c_out.at[:, k], c_dst.at[:, k], out_sem.at[4 + k]) for k in range(depth)]
+    u_out[...] = u2[:, PAD : PAD + ROWS, :]
+    v_out[...] = v2[:, PAD : PAD + ROWS, :]
+    saves[0].start()
+    saves[1].start()
+    t_base[...] = (wet * (t1 + 0.1 * lap(t1)))[:, PAD : PAD + ROWS, :]
+    wet_strip[...] = wet[:, PAD : PAD + ROWS, :]
+
     wide = tracers * ROWS
     spread = (
         lax.broadcasted_iota(jnp.int32, (wide, tracers), 0) // ROWS
@@ -208,77 +279,6 @@
     rates_hi = rates.astype(jnp.bfloat16)
     rates_lo = (rates - rates_hi.astype(F32)).astype(jnp.bfloat16)
 
-    zero = jnp.zeros((share, PAD, width), F32)
-    for f in range(4):
-        ext[f, :, 0:PAD, :] = zero
-        ext[f, :, PAD + ROWS :, :] = zero
-    ext_n[0:PAD, :] = jnp.zeros((PAD, width), jnp.int32)
-    ext_n[PAD + ROWS :, :] = jnp.zeros((PAD, width), jnp.int32)
-    for f, ref in enumerate((u_in, v_in, t_in, h_in)):
-        ext[f, :, PAD : PAD + ROWS, :] = ref[...]
-    ext_n[PAD : PAD + ROWS, :] = n_in[...]
-
-    wait_recv(dyn)
-    ext[0, :, 2:4, :] = rc_s[:, 3:5, :]
-    ext[1, :, 1:4, :] = rc_s[:, 0:3, :]
-    ext[2, :, 2:4, :] = rc_s[:, 5:7, :]
-    ext[3, :, 3:4, :] = rc_s[:, 7:8, :]
-    ext[0, :, 12:14, :] = rc_n[:, 0:2, :]
-    ext[1, :, 12:14, :] = rc_n[:, 2:4, :]
-    ext[2, :, 12:14, :] = rc_n[:, 4:6, :]
-    ext[3, :, 12:13, :] = rc_n[:, 6:7, :]
-    ext_n[2:4, :] = cnt_s[6:8, :]
-    ext_n[12:14, :] = cnt_n[0:2, :]
-
-    shape = (share, EXT, width)
-    level = col * share + lax.broadcasted_iota(jnp.int32, shape, 0)
-    wet = (level < ext_n[...][None]).astype(F32)
-    wet_u = wet * east(wet)
-    wet_v = wet * north(wet)
-    spot = (s * ROWS - PAD + lax.broadcasted_iota(jnp.int32, shape, 1)).astype(F32)
-    fcor = 0.3 * (2.0 * (spot + 0.5) / (nstrip * ROWS) - 1.0)
-
-    def advance(u, v, t):
-        new_u = wet_u * (u + 0.1 * lap(u) + fcor * v - 0.2 * (east(t) - t))
-        new_v = wet_v * (v + 0.1 * lap(v) - fcor * u - 0.2 * (north(t) - t))
-        return new_u, new_v
-
-    def publish(m, u, v):
-        for p in range(nlon):
-            lo = p * LANES
-            cols = slice(lo, lo + LANES)
-            v_edge = jnp.zeros((ROWS, LANES), F32)
-            u_edge = jnp.zeros((ROWS, LANES), F32)
-            for l in range(share):
-                f_send[m, p, l] = u[l, PAD : PAD + ROWS, cols]
-                f_send[m, p, share + l] = v[l, PAD : PAD + ROWS, cols]
-                v_edge = jnp.where(row == l, v[l, PAD - 1 : PAD, cols], v_edge)
-                if p:
-                    u_edge = jnp.where(lane == l, u[l, PAD : PAD + ROWS, lo - 1 : lo], u_edge)
-            f_send[m, p, 2 * share] = v_edge
-            f_send[m, p, 2 * share + 1] = u_edge
-        for c in faces(m):
-            c.start()
-        f_recv[m, col] = f_send[m, col]
-
-    u0, v0, t0 = ext[0], ext[1], ext[2]
-    u1, v1 = advance(u0, v0, t0)
-    publish(0, u1, v1)
-    t1 = wet * (t0 + 0.1 * lap(t0) + 0.5 * ext[3])
-    u2, v2 = advance(u1, v1, t1)
-    publish(1, u2, v2)
-    saves = [
-        pltpu.make_async_copy(a, b, out_sem.at[i])
-        for i, (a, b) in enumerate(((u_out, u_dst), (v_out, v_dst), (t_out, t_dst), (h_out, h_dst)))
-    ]
-    saves += [pltpu.make_async_copy(c_out.at[:, k], c_dst.at[:, k], out_sem.at[4 + k]) for k in range(depth)]
-    u_out[...] = u2[:, PAD : PAD + ROWS, :]
-    v_out[...] = v2[:, PAD : PAD + ROWS, :]
-    saves[0].start()
-    saves[1].start()
-    t_base[...] = (wet * (t1 + 0.1 * lap(t1)))[:, PAD : PAD + ROWS, :]
-    wet_strip[...] = wet[:, PAD : PAD + ROWS, :]
-
     depth_here = n_in[:, pl.ds(pl.multiple_of(col * LANES, LANES), LANES)]
 
     def tile_step(m, source, target):
@@ -328,49 +328,58 @@
                     c.start()
                 h_recv[m, col] = h_send[m, col]
 
-        groups = depth // PAIR
         held = {}
-        for g in range(groups + 1):
-            if g < groups:
-                if m:
-                    wait_recv(second(g))
-                levels = range(g * PAIR, (g + 1) * PAIR)
-                for k in levels:
-                    shine(k)
-                adv = [
-                    jnp.concatenate([light[k][0]] + [advect(k, t) for t in range(1, tracers)], axis=0)
-                    for k in levels
-                ]
-                hi = [a.astype(jnp.bfloat16) for a in adv]
-                lo = [(a - b.astype(F32)).astype(jnp.bfloat16) for a, b in zip(adv, hi)]
-                held[g] = (adv, jnp.concatenate(hi, axis=1), jnp.concatenate(lo, axis=1))
-            if g > 0:
-                adv, hi, lo = held.pop(g - 1)
-                r = (
-                    jnp.dot(rates_hi, hi, preferred_element_type=F32)
-                    + jnp.dot(rates_hi, lo, preferred_element_type=F32)
-                    + jnp.dot(rates_lo, hi, preferred_element_type=F32)
-                )
-                for n in range(PAIR):
-                    k = (g - 1) * PAIR + n
-                    _, wet_k, top = light[k]
-                    gain = r[:, n * LANES : (n + 1) * LANES].reshape(tracers, ROWS, LANES)
-                    new = wet_k * (adv[n].reshape(tracers, ROWS, LANES) + (0.5 * top) * gain)
-                    target[:, k] = new
-                    if m == 0:
-                        pack(1, k, new)
-                    else:
-                        saves[4 + k].start()
+
+        def fluxes(g):
+            if m:
+                wait_recv(second(g))
+            levels = range(g * PAIR, (g + 1) * PAIR)
+            for k in levels:
+                shine(k)
+            adv = [
+                jnp.concatenate([light[k][0]] + [advect(k, t) for t in range(1, tracers)], axis=0)
+                for k in levels
+            ]
+            hi = [a.astype(jnp.bfloat16) for a in adv]
+            lo = [(a - b.astype(F32)).astype(jnp.bfloat16) for a, b in zip(adv, hi)]
+            held[g] = (adv, jnp.concatenate(hi, axis=1), jnp.concatenate(lo, axis=1))
+
+        def products(g):
+            adv, hi, lo = held.pop(g)
+            r = (
+                jnp.dot(rates_hi, hi, preferred_element_type=F32)
+                + jnp.dot(rates_hi, lo, preferred_element_type=F32)
+                + jnp.dot(rates_lo, hi, preferred_element_type=F32)
+            )
+            for n in range(PAIR):
+                k = g * PAIR + n
+                _, wet_k, top = light[k]
+                gain = r[:, n * LANES : (n + 1) * LANES].reshape(tracers, ROWS, LANES)
+                new = wet_k * (adv[n].reshape(tracers, ROWS, LANES) + (0.5 * top) * gain)
+                target[:, k] = new
                 if m == 0:
-                    start(second(g - 1))
-
+                    pack(1, k, new)
+                else:
+                    saves[4 + k].start()
+            if m == 0:
+                start(second(g))
+
+        return fluxes, products
+
+    pairs = depth // PAIR
+    parts = [tile_step(0, c_in, c_mid), tile_step(1, c_mid, c_out)]
+    order = [(m, g) for m in range(2) for g in range(pairs)]
     wait_recv(first)
     for c in faces(0):
         c.wait_recv()
-    tile_step(0, c_in, c_mid)
-    for c in faces(1):
-        c.wait_recv()
-    tile_step(1, c_mid, c_out)
+    for n, (m, g) in enumerate(order):
+        if (m, g) == (1, 0):
+            for c in faces(1):
+                c.wait_recv()
+        parts[m][0](g)
+        if n:
+            parts[order[n - 1][0]][1](order[n - 1][1])
+    parts[1][1](pairs - 1)
 
     for c in heats(0):
         c.wait_recv()

time: 19.4 us -> 21.7 us (1.12)
  the two profiles are of different devices: /device:TPU:0 before, /device:TPU:1 now
where the time goes in v5:
time: 21.7 us; the launch traced here: 21.5 us
  Pallas kernels  20.9 us (96%)
  between operations  0.64 us (3%)
    pallas_call x1, Pallas kernels, shards(): pl.pallas_call(functools.partial(kernel, sizes), out_shape=(strip, strip,...  18.8 us
    pallas_call x1, Pallas kernels, shards(): pl.pallas_call(store, out_shape=(strip, strip, strip, strip, jax.ShapeDty...  2.11 us

profile of v5, /device:TPU:1, one launch (start us, length us, event | category | flops | bytes accessed | tf_op | source)
XLA Modules:
  0.0 21.5 jit_solution(7529500139053922698)
XLA Ops:
  0.6 18.8 %shard_map.110 = (f32[4,8,256]{2,1,0:T(8,128)}, f32[4,8,256]{2,1,0:T(8,128)}, f32[4,8,256]{2,1,0:T(8,128)}, f32[4,8,256]{2,1,0:T(8,128)}, f32[24,8,8,128]{3,2,1,0:T(8,128)}) custom-call(f32[4,8,256]{2,1,0:T(8,128)} %u_hbm.1, f32[4,8,256]{2,1,0:T(8,128)} %v_hbm.1, f32[4,8,256]{2,1,0:T(8,128)} %t_hbm.1, f32[4,8,256]{2,1,0:T(8,128)} %h_hbm.1, ...), custom_call_target="tpu_custom_call" | custom-call | tf_op jit(solution)/shard_map/pallas_call | solution.py:434
  19.4 2.1 %shard_map.111 = (f32[4,8,256]{2,1,0:T(8,128)}, f32[4,8,256]{2,1,0:T(8,128)}, f32[4,8,256]{2,1,0:T(8,128)}, f32[4,8,256]{2,1,0:T(8,128)}, f32[24,8,8,128]{3,2,1,0:T(8,128)}) custom-call(f32[4,8,256]{2,1,0:T(8,128)} %get-tuple-element.10.refs_0_, f32[4,8,256]{2,1,0:T(8,128)} %get-tuple-element.11.refs_1_, f32[4,8,256]{2,1,0:T(8,128)} %get-tuple-element.12.refs_2_, ...), custom_call_target="tpu_custom_call" | custom-call | tf_op jit(solution)/shard_map/pallas_call | solution.py:468
